TPU v7x, 32 devices: a whole 2x2x4 slice. The times are simulated.
32 devices in a mesh: groups: 2 (over y), wband: 2 (over core), tile: 8 (over z, x).
Axes of the slice: x: 2, y: 2, z: 4, core: 2. Of those that a mesh axis runs over, the one named last changes fastest.
Arguments:
- visibility: float32 [65536, 2], P(('groups', 'wband', 'tile')), parts along dimension 0, may hold values from -6 to 6
- plane_index: int32 [65536], P(('groups', 'wband', 'tile')), parts along dimension 0, may hold values from 0 to 63, as said below
- beam_index: int32 [65536], P(('groups', 'wband', 'tile')), parts along dimension 0, may hold values from 0 to 31
- strip_index: int32 [65536], P(('groups', 'wband', 'tile')), parts along dimension 0, may hold values from 0 to 7, as said below
- cell_row: int32 [65536], P(('groups', 'wband', 'tile')), parts along dimension 0, may hold values from 0 to 63
- cell_column: int32 [65536], P(('groups', 'wband', 'tile')), parts along dimension 0, may hold values from 0 to 8184
- phase_index: int32 [65536], P(('groups', 'wband', 'tile')), parts along dimension 0, may hold values from 0 to 63, as said below
- kernel_table: bfloat16 [64, 32, 64, 128], P('wband', None, 'tile'), may hold values from -6 to 6
Outputs:
- grid: float32 [2, 1024, 8192], P(None, ('groups', 'tile'), 'wband'), parts along dimension 1
There are 2 independent parts, one for each index of `groups`. A program takes and returns all parts, laid end to end along the dimension named above; an argument that names none is the same for every part. Nothing has to cross between parts.
Inputs may be any that keep to these rules, and one draw needn't show every extreme that they name: `plane_index`: the blocks at wband index b have w-planes from b * 32 to (b + 1) * 32 - 1. `strip_index`: among the 2048 blocks of one device, at most 512 land in any one strip. `phase_index`: among the 2048 blocks of one device, at most 64 have any one phase.
All inputs are finite; a program needn't handle non-finite values.
Results may differ from a plain program's by a relative error of at most 0.003.
Values may be sent and summed in bfloat16 or wider, within the bound.
A program may use at most 192 MiB of HBM per device.

v0:
```python
import math

import jax
import jax.numpy as jnp
from jax import lax
from jax.sharding import PartitionSpec as P

SUP = 8
NV = 8192
ROWS = 64


def from_behind(block, axis, distance):
    devices = range(lax.axis_size(axis))
    route = [(i - distance, i) for i in devices if i - distance in devices]
    return lax.ppermute(block, axis, route)


def make_patches(values, kernel_rows):
    widened = kernel_rows.astype(jnp.float32)
    halfway = widened.shape[1] // 2
    real_kernel = widened[:, :halfway]
    imag_kernel = widened[:, halfway:]
    real_value = values[:, 0:1]
    imag_value = values[:, 1:2]
    real_part = real_value * real_kernel - imag_value * imag_kernel
    imag_part = real_value * imag_kernel + imag_value * real_kernel
    return jnp.concatenate([real_part, imag_part], axis=1).astype(jnp.bfloat16)


def slot_positions(target, buckets, capacity):
    onehot = (target[:, None] == jnp.arange(buckets, dtype=jnp.int32)[None, :]).astype(jnp.int32)
    ranking = jnp.cumsum(onehot, axis=0) - 1
    return target * capacity + jnp.sum(ranking * onehot, axis=1)


def paint(patches, row_start, col_start, columns, height, width):
    support = SUP
    lanes = 128
    block_count = columns // lanes
    total = patches.shape[0]
    group = math.gcd(total, 512)
    patch_grid = patches.reshape(total, 2, support, support)
    across = jnp.arange(support, dtype=jnp.int32)
    row_axis = jnp.arange(height, dtype=jnp.int32)
    lane_axis = jnp.arange(lanes + support, dtype=jnp.int32)
    block_axis = jnp.arange(block_count, dtype=jnp.int32)

    def add_group(number, totals):
        first = number * group
        piece = lax.dynamic_slice_in_dim(patch_grid, first, group, 0)
        rows_here = lax.dynamic_slice_in_dim(row_start, first, group, 0)
        cols_here = lax.dynamic_slice_in_dim(col_start, first, group, 0)
        block_here = cols_here // lanes
        offset_here = cols_here % lanes
        row_select = (
            row_axis[None, :, None] == rows_here[:, None, None] + across[None, None, :]
        ).astype(jnp.bfloat16)
        lane_select = (
            lane_axis[None, None, :] == offset_here[:, None, None] + across[None, :, None]
        ).astype(jnp.bfloat16)
        block_select = (block_here[:, None] == block_axis[None, :]).astype(jnp.bfloat16)
        placed = jnp.einsum(
            "gkij,gjw->gkiw", piece, lane_select, preferred_element_type=jnp.float32
        ).astype(jnp.bfloat16)
        lifted = jnp.einsum(
            "gti,gkiw->gktw", row_select, placed, preferred_element_type=jnp.float32
        ).astype(jnp.bfloat16)
        return totals + jnp.einsum(
            "gb,gktw->ktbw", block_select, lifted, preferred_element_type=jnp.float32
        )

    totals = jnp.zeros((2, height, block_count, lanes + support), jnp.float32)
    totals = lax.fori_loop(0, total // group, add_group, totals)
    canvas = jnp.zeros((2, height, block_count + 1, lanes), jnp.float32)
    canvas = canvas.at[:, :, :block_count, :].add(totals[..., :lanes])
    canvas = canvas.at[:, :, 1:, :support].add(totals[..., lanes:])
    return canvas.reshape(2, height, (block_count + 1) * lanes)[:, :, :width]


def local(
    visibility,
    plane_index,
    beam_index,
    strip_index,
    cell_row,
    cell_column,
    phase_index,
    kernel_table,
):
    blocks = visibility.shape[0]
    strips = lax.axis_size("tile")
    planes_band = kernel_table.shape[0]
    beam_count = kernel_table.shape[1]
    phase_local = kernel_table.shape[2]
    row_width = kernel_table.shape[3]
    phases = phase_local * strips
    band_index = lax.axis_index("wband")
    kernel_key = (plane_index - band_index * planes_band) * beam_count + beam_index
    gathered = lax.all_gather(kernel_table, "tile", axis=2, tiled=True)
    lookup = kernel_key * phases + phase_index
    patches = make_patches(visibility, gathered.reshape(-1, row_width)[lookup])
    strip_capacity = 2 * blocks // strips
    height = ROWS + SUP - 1
    places = slot_positions(strip_index, strips, strip_capacity)
    outgoing_patches = (
        jnp.zeros((strips * strip_capacity, row_width), jnp.bfloat16).at[places].set(patches)
    )
    outgoing_cells = (
        jnp.zeros((strips * strip_capacity,), jnp.int32).at[places].set(cell_row * NV + cell_column)
    )
    incoming_patches, incoming_cells = (
        lax.all_to_all(outgoing_patches, "tile", split_axis=0, concat_axis=0, tiled=True),
        lax.all_to_all(outgoing_cells, "tile", split_axis=0, concat_axis=0, tiled=True),
    )
    canvas = paint(incoming_patches, incoming_cells // NV, incoming_cells % NV, NV, height, NV)
    spilled = from_behind(canvas[:, ROWS:, :], "tile", 1)
    strip_grid = canvas[:, :ROWS, :].at[:, : SUP - 1, :].add(spilled)
    result = lax.psum_scatter(strip_grid, "wband", scatter_dimension=2, tiled=True)
    return result


def solution(mesh):
    placed = (
        P(("groups", "wband", "tile"), None),
        P(("groups", "wband", "tile")),
        P(("groups", "wband", "tile")),
        P(("groups", "wband", "tile")),
        P(("groups", "wband", "tile")),
        P(("groups", "wband", "tile")),
        P(("groups", "wband", "tile")),
        P("wband", None, "tile", None),
    )
    return jax.shard_map(
        local,
        mesh=mesh,
        in_specs=placed,
        out_specs=P(None, ("groups", "tile"), "wband"),
        check_vma=False,
    )
```

profile of v0, /device:TPU:0, one launch (start us, length us, event | category | flops | bytes accessed | tf_op | source)
XLA Modules:
  0.0 1072.2 jit_solution(14042986862607321323)
XLA Ops:
  8.0 2.3 reduce-window.6
  12.3 8.6 scatter_custom_fusion.1
  20.9 7.3 all-to-all-start.1
  29.7 210.4 %all-gather.2.cloned.1.call-done = bf16[32,32,64,128]{3,2,1,0:T(8,128)(2,1)} async-done(((bf16[32,32,8,128]{3,2,1,0:T(8,128)(2,1)}), bf16[32,32,64,128]{3,2,1,0:T(8,128)(2,1)}) %all-gather.2.cloned.1.call-update) | async-done | bytes 16777232 | tf_op jit(solution)/shard_map/all_gather | solution.py:100
  240.1 13.5 %gather_fusion = bf16[2048,128]{1,0:T(8,128)(2,1)S(1)} fusion(bf16[65536,128]{1,0:T(8,128)(2,1)} %bitcast.59, s32[2048]{0:T(1024)S(1)} %fusion.39), kind=kCustom, calls=%fused_computation | custom fusion | bytes 1056768 | tf_op jit(solution)/shard_map/gather | solution.py:102
  254.7 6.5 scatter_custom_fusion
  261.2 1.3 copy.17
  262.5 3.6 all-to-all-start
  266.3 25.3 %all-to-all-done = bf16[8,512,128]{1,2,0:T(8,128)(2,1)S(1)} async-done(((bf16[8,512,128]{1,2,0:T(8,128)(2,1)}), bf16[8,512,128]{1,2,0:T(8,128)(2,1)S(1)}, u32[]{:S(2)}, u32[]{:S(2)}) %all-to-all-start) | async-done | bytes 1048608 | tf_op jit(solution)/shard_map/all_to_all | solution.py:113
  292.3 20.0 %reshape.238 = bf16[4096,2,8,8]{3,2,1,0:T(8,128)(2,1)} reshape(bf16[8,512,128]{2,1,0:T(8,128)(2,1)S(1)} %copy.24) | data formatting | bytes 2097152
  312.3 664.1 %while.20 = (s32[]{:T(128)}, f32[2,71,64,136]{3,2,1,0:T(8,128)}, bf16[4096,2,8,8]{3,2,1,0:T(8,128)(2,1)}, s32[4096]{0:T(1024)S(1)}, s32[4096]{0:T(1024)S(1)}, /*index=5*/s32[]{:T(128)}, s32[]{:T(128)}, s32[]{:T(128)}, s32[]{:T(128)}) while((s32[]{:T(128)}, f32[2,71,64,136]{3,2,1,0:T(8,128)}, ...), condition=%wide.region_6.7_spmd.clone.clone, body=%wide.region_5.6_spmd.clone.clone.sunk | while | flops 1456033280 | bytes 91168928 | solution.py:74
  312.7 17.0 %convert_bitcast_fusion.2 = bf16[512,2,71,136]{2,3,1,0:T(8,128)(2,1)} fusion(s32[512,8]{1,0:T(8,128)S(1)} %get-tuple-element.384, bf16[4096,2,8,8]{3,2,1,0:T(8,128)(2,1)} %get-tuple-element.407, s32[]{:T(128)S(6)} %select_n.83, s32[512,8]{1,0:T(8,128)S(1)} %get-tuple-element.385), kind=kOutput, calls=%fused_computation.7.clone.1 | convolution fusion | flops 187879424 | bytes 21905412 | tf_op jit(solution)/shard_map/while/body/eval_jaxpr/gti,gkiw->gktw/dot_general | solution.py:66
  329.7 47.8 %copy.29 = bf16[512,2,71,136]{0,3,2,1:T(8,128)(2,1)} copy(bf16[512,2,71,136]{2,3,1,0:T(8,128)(2,1)} %convert_bitcast_fusion.2) | data formatting | bytes 39550976 | tf_op jit(solution)/shard_map/while/body/eval_jaxpr/convert_element_type | solution.py:68
  377.5 15.4 %bitcast_add_fusion.2 = f32[2,71,64,136]{3,2,1,0:T(8,128)} fusion(f32[2,71,64,136]{3,2,1,0:T(8,128)} %get-tuple-element.397, pred[]{:T(512)S(6)} %compare.35, bf16[512,2,71,136]{0,3,2,1:T(8,128)(2,1)} %copy.29, s32[512]{0:T(512)S(1)} %get-tuple-element.386), kind=kOutput, calls=%fused_computation.8.clone.1 | convolution fusion | flops 1268135936 | bytes 29665280 | tf_op jit(solution)/shard_map/while/body/eval_jaxpr/gb,gktw->ktbw/dot_general | solution.py:69
  393.2 17.0 %convert_bitcast_fusion.2 = bf16[512,2,71,136]{2,3,1,0:T(8,128)(2,1)} fusion(s32[512,8]{1,0:T(8,128)S(1)} %get-tuple-element.384, bf16[4096,2,8,8]{3,2,1,0:T(8,128)(2,1)} %get-tuple-element.407, s32[]{:T(128)S(6)} %select_n.83, s32[512,8]{1,0:T(8,128)S(1)} %get-tuple-element.385), kind=kOutput, calls=%fused_computation.7.clone.1 | convolution fusion | flops 187879424 | bytes 21905412 | tf_op jit(solution)/shard_map/while/body/eval_jaxpr/gti,gkiw->gktw/dot_general | solution.py:66
  410.3 47.8 %copy.29 = bf16[512,2,71,136]{0,3,2,1:T(8,128)(2,1)} copy(bf16[512,2,71,136]{2,3,1,0:T(8,128)(2,1)} %convert_bitcast_fusion.2) | data formatting | bytes 39550976 | tf_op jit(solution)/shard_map/while/body/eval_jaxpr/convert_element_type | solution.py:68
  458.1 18.1 %bitcast_add_fusion.2 = f32[2,71,64,136]{3,2,1,0:T(8,128)} fusion(f32[2,71,64,136]{3,2,1,0:T(8,128)} %get-tuple-element.397, pred[]{:T(512)S(6)} %compare.35, bf16[512,2,71,136]{0,3,2,1:T(8,128)(2,1)} %copy.29, s32[512]{0:T(512)S(1)} %get-tuple-element.386), kind=kOutput, calls=%fused_computation.8.clone.1 | convolution fusion | flops 1268135936 | bytes 29665280 | tf_op jit(solution)/shard_map/while/body/eval_jaxpr/gb,gktw->ktbw/dot_general | solution.py:69
  476.6 17.0 %convert_bitcast_fusion.2 = bf16[512,2,71,136]{2,3,1,0:T(8,128)(2,1)} fusion(s32[512,8]{1,0:T(8,128)S(1)} %get-tuple-element.384, bf16[4096,2,8,8]{3,2,1,0:T(8,128)(2,1)} %get-tuple-element.407, s32[]{:T(128)S(6)} %select_n.83, s32[512,8]{1,0:T(8,128)S(1)} %get-tuple-element.385), kind=kOutput, calls=%fused_computation.7.clone.1 | convolution fusion | flops 187879424 | bytes 21905412 | tf_op jit(solution)/shard_map/while/body/eval_jaxpr/gti,gkiw->gktw/dot_general | solution.py:66
  493.6 47.8 %copy.29 = bf16[512,2,71,136]{0,3,2,1:T(8,128)(2,1)} copy(bf16[512,2,71,136]{2,3,1,0:T(8,128)(2,1)} %convert_bitcast_fusion.2) | data formatting | bytes 39550976 | tf_op jit(solution)/shard_map/while/body/eval_jaxpr/convert_element_type | solution.py:68
  541.4 18.1 %bitcast_add_fusion.2 = f32[2,71,64,136]{3,2,1,0:T(8,128)} fusion(f32[2,71,64,136]{3,2,1,0:T(8,128)} %get-tuple-element.397, pred[]{:T(512)S(6)} %compare.35, bf16[512,2,71,136]{0,3,2,1:T(8,128)(2,1)} %copy.29, s32[512]{0:T(512)S(1)} %get-tuple-element.386), kind=kOutput, calls=%fused_computation.8.clone.1 | convolution fusion | flops 1268135936 | bytes 29665280 | tf_op jit(solution)/shard_map/while/body/eval_jaxpr/gb,gktw->ktbw/dot_general | solution.py:69
  560.0 17.0 %convert_bitcast_fusion.2 = bf16[512,2,71,136]{2,3,1,0:T(8,128)(2,1)} fusion(s32[512,8]{1,0:T(8,128)S(1)} %get-tuple-element.384, bf16[4096,2,8,8]{3,2,1,0:T(8,128)(2,1)} %get-tuple-element.407, s32[]{:T(128)S(6)} %select_n.83, s32[512,8]{1,0:T(8,128)S(1)} %get-tuple-element.385), kind=kOutput, calls=%fused_computation.7.clone.1 | convolution fusion | flops 187879424 | bytes 21905412 | tf_op jit(solution)/shard_map/while/body/eval_jaxpr/gti,gkiw->gktw/dot_general | solution.py:66
  577.0 47.8 %copy.29 = bf16[512,2,71,136]{0,3,2,1:T(8,128)(2,1)} copy(bf16[512,2,71,136]{2,3,1,0:T(8,128)(2,1)} %convert_bitcast_fusion.2) | data formatting | bytes 39550976 | tf_op jit(solution)/shard_map/while/body/eval_jaxpr/convert_element_type | solution.py:68
  624.8 18.1 %bitcast_add_fusion.2 = f32[2,71,64,136]{3,2,1,0:T(8,128)} fusion(f32[2,71,64,136]{3,2,1,0:T(8,128)} %get-tuple-element.397, pred[]{:T(512)S(6)} %compare.35, bf16[512,2,71,136]{0,3,2,1:T(8,128)(2,1)} %copy.29, s32[512]{0:T(512)S(1)} %get-tuple-element.386), kind=kOutput, calls=%fused_computation.8.clone.1 | convolution fusion | flops 1268135936 | bytes 29665280 | tf_op jit(solution)/shard_map/while/body/eval_jaxpr/gb,gktw->ktbw/dot_general | solution.py:69
  643.3 17.0 %convert_bitcast_fusion.2 = bf16[512,2,71,136]{2,3,1,0:T(8,128)(2,1)} fusion(s32[512,8]{1,0:T(8,128)S(1)} %get-tuple-element.384, bf16[4096,2,8,8]{3,2,1,0:T(8,128)(2,1)} %get-tuple-element.407, s32[]{:T(128)S(6)} %select_n.83, s32[512,8]{1,0:T(8,128)S(1)} %get-tuple-element.385), kind=kOutput, calls=%fused_computation.7.clone.1 | convolution fusion | flops 187879424 | bytes 21905412 | tf_op jit(solution)/shard_map/while/body/eval_jaxpr/gti,gkiw->gktw/dot_general | solution.py:66
  660.3 47.8 %copy.29 = bf16[512,2,71,136]{0,3,2,1:T(8,128)(2,1)} copy(bf16[512,2,71,136]{2,3,1,0:T(8,128)(2,1)} %convert_bitcast_fusion.2) | data formatting | bytes 39550976 | tf_op jit(solution)/shard_map/while/body/eval_jaxpr/convert_element_type | solution.py:68
  708.1 18.1 %bitcast_add_fusion.2 = f32[2,71,64,136]{3,2,1,0:T(8,128)} fusion(f32[2,71,64,136]{3,2,1,0:T(8,128)} %get-tuple-element.397, pred[]{:T(512)S(6)} %compare.35, bf16[512,2,71,136]{0,3,2,1:T(8,128)(2,1)} %copy.29, s32[512]{0:T(512)S(1)} %get-tuple-element.386), kind=kOutput, calls=%fused_computation.8.clone.1 | convolution fusion | flops 1268135936 | bytes 29665280 | tf_op jit(solution)/shard_map/while/body/eval_jaxpr/gb,gktw->ktbw/dot_general | solution.py:69
  726.7 17.0 %convert_bitcast_fusion.2 = bf16[512,2,71,136]{2,3,1,0:T(8,128)(2,1)} fusion(s32[512,8]{1,0:T(8,128)S(1)} %get-tuple-element.384, bf16[4096,2,8,8]{3,2,1,0:T(8,128)(2,1)} %get-tuple-element.407, s32[]{:T(128)S(6)} %select_n.83, s32[512,8]{1,0:T(8,128)S(1)} %get-tuple-element.385), kind=kOutput, calls=%fused_computation.7.clone.1 | convolution fusion | flops 187879424 | bytes 21905412 | tf_op jit(solution)/shard_map/while/body/eval_jaxpr/gti,gkiw->gktw/dot_general | solution.py:66
  743.7 47.8 %copy.29 = bf16[512,2,71,136]{0,3,2,1:T(8,128)(2,1)} copy(bf16[512,2,71,136]{2,3,1,0:T(8,128)(2,1)} %convert_bitcast_fusion.2) | data formatting | bytes 39550976 | tf_op jit(solution)/shard_map/while/body/eval_jaxpr/convert_element_type | solution.py:68
  791.5 18.1 %bitcast_add_fusion.2 = f32[2,71,64,136]{3,2,1,0:T(8,128)} fusion(f32[2,71,64,136]{3,2,1,0:T(8,128)} %get-tuple-element.397, pred[]{:T(512)S(6)} %compare.35, bf16[512,2,71,136]{0,3,2,1:T(8,128)(2,1)} %copy.29, s32[512]{0:T(512)S(1)} %get-tuple-element.386), kind=kOutput, calls=%fused_computation.8.clone.1 | convolution fusion | flops 1268135936 | bytes 29665280 | tf_op jit(solution)/shard_map/while/body/eval_jaxpr/gb,gktw->ktbw/dot_general | solution.py:69
  810.0 17.0 %convert_bitcast_fusion.2 = bf16[512,2,71,136]{2,3,1,0:T(8,128)(2,1)} fusion(s32[512,8]{1,0:T(8,128)S(1)} %get-tuple-element.384, bf16[4096,2,8,8]{3,2,1,0:T(8,128)(2,1)} %get-tuple-element.407, s32[]{:T(128)S(6)} %select_n.83, s32[512,8]{1,0:T(8,128)S(1)} %get-tuple-element.385), kind=kOutput, calls=%fused_computation.7.clone.1 | convolution fusion | flops 187879424 | bytes 21905412 | tf_op jit(solution)/shard_map/while/body/eval_jaxpr/gti,gkiw->gktw/dot_general | solution.py:66
  827.0 47.8 %copy.29 = bf16[512,2,71,136]{0,3,2,1:T(8,128)(2,1)} copy(bf16[512,2,71,136]{2,3,1,0:T(8,128)(2,1)} %convert_bitcast_fusion.2) | data formatting | bytes 39550976 | tf_op jit(solution)/shard_map/while/body/eval_jaxpr/convert_element_type | solution.py:68
  874.9 18.1 %bitcast_add_fusion.2 = f32[2,71,64,136]{3,2,1,0:T(8,128)} fusion(f32[2,71,64,136]{3,2,1,0:T(8,128)} %get-tuple-element.397, pred[]{:T(512)S(6)} %compare.35, bf16[512,2,71,136]{0,3,2,1:T(8,128)(2,1)} %copy.29, s32[512]{0:T(512)S(1)} %get-tuple-element.386), kind=kOutput, calls=%fused_computation.8.clone.1 | convolution fusion | flops 1268135936 | bytes 29665280 | tf_op jit(solution)/shard_map/while/body/eval_jaxpr/gb,gktw->ktbw/dot_general | solution.py:69
  893.4 17.0 %convert_bitcast_fusion.2 = bf16[512,2,71,136]{2,3,1,0:T(8,128)(2,1)} fusion(s32[512,8]{1,0:T(8,128)S(1)} %get-tuple-element.384, bf16[4096,2,8,8]{3,2,1,0:T(8,128)(2,1)} %get-tuple-element.407, s32[]{:T(128)S(6)} %select_n.83, s32[512,8]{1,0:T(8,128)S(1)} %get-tuple-element.385), kind=kOutput, calls=%fused_computation.7.clone.1 | convolution fusion | flops 187879424 | bytes 21905412 | tf_op jit(solution)/shard_map/while/body/eval_jaxpr/gti,gkiw->gktw/dot_general | solution.py:66
  910.4 47.8 %copy.29 = bf16[512,2,71,136]{0,3,2,1:T(8,128)(2,1)} copy(bf16[512,2,71,136]{2,3,1,0:T(8,128)(2,1)} %convert_bitcast_fusion.2) | data formatting | bytes 39550976 | tf_op jit(solution)/shard_map/while/body/eval_jaxpr/convert_element_type | solution.py:68
  958.2 18.1 %bitcast_add_fusion.2 = f32[2,71,64,136]{3,2,1,0:T(8,128)} fusion(f32[2,71,64,136]{3,2,1,0:T(8,128)} %get-tuple-element.397, pred[]{:T(512)S(6)} %compare.35, bf16[512,2,71,136]{0,3,2,1:T(8,128)(2,1)} %copy.29, s32[512]{0:T(512)S(1)} %get-tuple-element.386), kind=kOutput, calls=%fused_computation.8.clone.1 | convolution fusion | flops 1268135936 | bytes 29665280 | tf_op jit(solution)/shard_map/while/body/eval_jaxpr/gb,gktw->ktbw/dot_general | solution.py:69
  976.4 2.8 slice.125
  979.2 2.2 copy-done
  981.4 3.1 slice_add_fusion
  984.5 2.8 scatter-add.10
  987.3 41.4 %scatter-add.11 = f32[2,71,65,128]{3,2,1,0:T(8,128)} dynamic-update-slice(f32[2,71,65,128]{3,2,1,0:T(8,128)} %scatter-add.10, f32[2,71,64,8]{3,2,1,0:T(8,128)} %slice_add_fusion, s32[]{:T(128)} %constant.217.clone.1, s32[]{:T(128)} %constant.217.clone.1, s32[]{:T(128)} %constant.229.clone.1, s32[]{:T(128)} %constant.217.clone.1) | dynamic-update-slice | bytes 581636 | tf_op jit(solution)/shard_map/scatter-add | solution.py:77
  1028.7 4.4 reshape.207
  1033.1 1.1 slice.138
  1034.2 3.3 collective-permute-start
  1037.5 4.5 slice.136
  1042.0 5.8 collective-permute-done
  1047.8 1.1 slice_add_fusion.1
  1048.9 3.4 scatter-add.14
  1052.4 13.0 %reduce-scatter.2.cloned.1.call-done = f32[2,64,4096]{2,1,0:T(8,128)} async-done(((f32[2,64,8192]{2,1,0:T(8,128)}), f32[2,64,4096]{2,1,0:T(8,128)}) %reduce-scatter.2.cloned.1.call-update) | async-done | bytes 2097168 | tf_op jit(solution)/shard_map/reduce_scatter | solution.py:119
  (43 shorter events, 9.8 us)
Async XLA Ops:
  6.5 233.5 %all-gather.2.cloned.1.call-start = ((), (), s32[]{:S(2)}) async-start(), calls=%async_computation.3 | async-start | bytes 18874368 | tf_op jit(solution)/shard_map/all_gather | solution.py:100
  20.9 241.6 %all-to-all-start.1 = ((s32[8,512,1]{1,2,0:T(1,128)}), s32[8,512,1]{1,2,0:T(1,128)S(1)}, u32[]{:S(2)}, u32[]{:S(2)}) async-start(s32[8,512,1]{1,2,0:T(1,128)} %bitcast.6), calls=%async_computation.1 | async-start | bytes 32768 | tf_op jit(solution)/shard_map/all_to_all | solution.py:114
  262.5 29.1 %all-to-all-start = ((bf16[8,512,128]{1,2,0:T(8,128)(2,1)}), bf16[8,512,128]{1,2,0:T(8,128)(2,1)S(1)}, u32[]{:S(2)}, u32[]{:S(2)}) async-start(bf16[8,512,128]{1,2,0:T(8,128)(2,1)} %copy.17), calls=%async_computation | async-start | bytes 2097152 | tf_op jit(solution)/shard_map/all_to_all | solution.py:113
  266.1 799.3 %reduce-scatter.2.cloned.1.call-start = ((), (), s32[]{:S(2)}) async-start(), calls=%async_computation.4 | async-start | bytes 6291456 | tf_op jit(solution)/shard_map/reduce_scatter | solution.py:119
  976.3 5.0 copy-start
  1034.2 13.6 %collective-permute-start = (f32[2,7,8192]{2,1,0:T(8,128)S(1)}, f32[2,7,8192]{2,1,0:T(8,128)S(1)}, u32[]{:S(2)}, u32[]{:S(2)}) collective-permute-start(f32[2,7,8192]{2,1,0:T(8,128)S(1)} %slice.138), channel_id=1, source_target_pairs={{0,1},{1,2},{2,3},{3,4},{4,5},{5,6},{6,7},{8,9},{9,10},{10,11},{11... | collective-permute-start | bytes 1376264 | tf_op jit(solution)/shard_map/ppermute | solution.py:16
Sparse Core Ops, SparseCore 0:
  9.4 230.6 all-gather.1
  1052.5 12.8 reduce-scatter.1
where the time goes:
time: 1080 us; the launch traced here: 1070 us
  local copies, waits for them, and re-layouts  491 us (45%)
  matrix products  279 us (26%)
  waiting for transfers between devices  255 us (24%)
  other arithmetic  19.5 us (2%)
  starting transfers between devices  14.3 us (1%)
  between operations  13.5 us (1%)
    convert_element_type x8, local copies, waits for them, and re-layouts, add_group(): lifted = jnp.einsum('gti,gkiw->gktw', row_select, placed, preferred_eleme...  383 us
    all_gather x1, waiting for transfers between devices, local(): gathered = lax.all_gather(kernel_table, 'tile', axis=2, tiled=True)  210 us
    dot_general x8, matrix products, add_group(): jnp.einsum('gb,gktw->ktbw', block_select, lifted, preferred_element_type=...  142 us
    dot_general x8, matrix products, add_group(): jnp.einsum('gti,gkiw->gktw', row_select, placed, preferred_element_type=j...  136 us
    scatter-add x1, local copies, waits for them, and re-layouts, paint(): canvas = canvas.at[:, :, 1:, :support].add(totals[..., lanes:])  41.4 us
    all_to_all x1, waiting for transfers between devices, local(): lax.all_to_all(outgoing_patches, 'tile', split_axis=0, concat_axis=0, til...  25.3 us
    unnamed x4, local copies, waits for them, and re-layouts  22.8 us
  transfers between devices with their start and end apart: 5, of which 4 were waited for; matrix products, arithmetic and copies ran while one was open for 4% of the time, Pallas kernels for 0%

commit v1 on v0

v1 whole, which is shorter than its diff:
```python
import functools

import jax
import jax.numpy as jnp
from jax import lax
from jax.experimental import pallas as pl
from jax.experimental.pallas import tpu as pltpu
from jax.sharding import PartitionSpec as P

SUP = 8
NV = 8192
ROWS = 64
LANES = 128
HALF = LANES // 2
SHIFT = 5
STRIDE = 1 << SHIFT
HEIGHT = ROWS + SUP
TILES = NV // STRIDE + 1
CHAINS = 2


def rank_in_bucket(target, buckets):
    onehot = (target[:, None] == jnp.arange(buckets, dtype=jnp.int32)[None, :]).astype(jnp.int32)
    ranking = jnp.cumsum(onehot, axis=0) - 1
    return jnp.sum(ranking * onehot, axis=1)


def fetch_kernel(unroll, keys_ref, table_ref, out_ref, wide, picked):
    wide[...] = table_ref[...].astype(jnp.float32)

    def body(i, carry):
        for u in range(unroll):
            n = i * unroll + u
            picked[pl.ds(n, 1), :] = wide[pl.ds(keys_ref[n], 1), :]
        return carry

    lax.fori_loop(0, out_ref.shape[0] // unroll, body, 0)
    out_ref[...] = picked[...].astype(jnp.bfloat16)


def fetch_rows(keys, table):
    total, width = keys.shape[0], table.shape[1]
    return pl.pallas_call(
        functools.partial(fetch_kernel, 16),
        out_shape=jax.ShapeDtypeStruct((total, width), jnp.bfloat16),
        in_specs=[
            pl.BlockSpec(memory_space=pltpu.SMEM),
            pl.BlockSpec(memory_space=pltpu.VMEM),
        ],
        out_specs=pl.BlockSpec(memory_space=pltpu.VMEM),
        scratch_shapes=[
            pltpu.VMEM(table.shape, jnp.float32),
            pltpu.VMEM((total, width), jnp.float32),
        ],
        compiler_params=pltpu.CompilerParams(vmem_limit_bytes=40 * 2**20),
        name="fetch_rows",
    )(keys, table)


def patch_kernel(unroll, source_ref, place_ref, real_ref, imag_ref, rows_ref, out_ref, straight, turned, made):
    wide = rows_ref[...].astype(jnp.float32)
    straight[...] = wide
    lane = lax.broadcasted_iota(jnp.int32, wide.shape, 1)
    swapped = pltpu.roll(wide, HALF, 1)
    turned[...] = jnp.where(lane < HALF, -swapped, swapped)
    made[...] = jnp.zeros_like(made)

    def body(i, carry):
        for u in range(unroll):
            n = i * unroll + u
            row = pl.ds(source_ref[n], 1)
            made[pl.ds(place_ref[n], 1), :] = (
                real_ref[n] * straight[row, :] + imag_ref[n] * turned[row, :]
            )
        return carry

    lax.fori_loop(0, source_ref.shape[0] // unroll, body, 0)
    out_ref[...] = made[...].astype(jnp.bfloat16)


def place_patches(source, place, visibility, rows, slots):
    width = rows.shape[1]
    smem = pl.BlockSpec(memory_space=pltpu.SMEM)
    vmem = pl.BlockSpec(memory_space=pltpu.VMEM)
    return pl.pallas_call(
        functools.partial(patch_kernel, 16),
        out_shape=jax.ShapeDtypeStruct((slots, width), jnp.bfloat16),
        in_specs=[smem, smem, smem, smem, vmem],
        out_specs=vmem,
        scratch_shapes=[
            pltpu.VMEM(rows.shape, jnp.float32),
            pltpu.VMEM(rows.shape, jnp.float32),
            pltpu.VMEM((slots, width), jnp.float32),
        ],
        compiler_params=pltpu.CompilerParams(vmem_limit_bytes=40 * 2**20),
        name="place_patches",
    )(source, place, visibility[:, 0], visibility[:, 1], rows)


def paint_kernel(
    unroll, cells_ref, band_ref, patches_ref, own_ref, own_edge_ref, other_ref, other_edge_ref, wide, *canvases
):
    source = lax.broadcasted_iota(jnp.int32, (LANES, LANES), 0)
    target = lax.broadcasted_iota(jnp.int32, (LANES, LANES), 1)
    picks = [
        ((source == target + s * SUP) & (target % HALF < SUP)).astype(jnp.bfloat16) for s in range(SUP)
    ]

    def open_out(i, carry):
        first = pl.multiple_of(i * LANES, LANES)
        part = patches_ref[pl.ds(first, LANES), :]
        for s in range(SUP):
            wide[pl.ds(first * SUP + s, LANES, stride=SUP), :] = jnp.dot(
                part, picks[s], preferred_element_type=jnp.float32
            )
        return carry

    lax.fori_loop(0, patches_ref.shape[0] // LANES, open_out, 0)

    def clear(i, carry):
        start = pl.multiple_of(i * HEIGHT, SUP)
        for canvas in canvases:
            canvas[pl.ds(start, HEIGHT), :] = jnp.zeros((HEIGHT, LANES), jnp.float32)
        return carry

    lax.fori_loop(0, TILES, clear, 0)

    lane = lax.broadcasted_iota(jnp.int32, (SUP, LANES), 1)

    def body(i, carry):
        spread = []
        for u in range(unroll):
            n = i * unroll + u
            cell = cells_ref[n]
            patch = wide[pl.ds(pl.multiple_of(n * SUP, SUP), SUP), :]
            spread.append((cell >> SHIFT, pltpu.roll(patch, cell & (STRIDE - 1), 1)))
        for u, (start, moved) in enumerate(spread):
            canvas = canvases[u % len(canvases)]
            canvas[pl.ds(start, SUP), :] = canvas[pl.ds(start, SUP), :] + moved
        return carry

    lax.fori_loop(0, patches_ref.shape[0] // unroll, body, 0)

    per_block = LANES // STRIDE
    blocks = NV // LANES // 2
    lower = lane < HALF
    quarter = (lane % HALF) < STRIDE
    middle = (lane >= STRIDE) & (lane < LANES - STRIDE)

    def merge(start_block, main_ref, edge_ref):
        def column(b, carry):
            first = (start_block + b) * per_block
            at = pl.ds(pl.multiple_of(b * LANES, LANES), LANES)
            for p in range(HEIGHT // SUP):
                tiles = []
                for t in range(per_block + 1):
                    where = pl.ds(pl.multiple_of((first + t) * HEIGHT + p * SUP, SUP), SUP)
                    tile = canvases[0][where, :]
                    for canvas in canvases[1:]:
                        tile = tile + canvas[where, :]
                    tiles.append(tile)
                before, t0, t1, t2, t3 = tiles
                edges = jnp.where(quarter, t3, before)
                real = jnp.where(lower, t0, pltpu.roll(t2, HALF, 1)) + jnp.where(
                    middle, pltpu.roll(t1, STRIDE, 1), pltpu.roll(edges, LANES - STRIDE, 1)
                )
                imag = jnp.where(lower, pltpu.roll(t0, HALF, 1), t2) + jnp.where(
                    middle, pltpu.roll(t1, LANES - STRIDE, 1), pltpu.roll(edges, STRIDE, 1)
                )
                if p < ROWS // SUP:
                    rows = slice(p * SUP, (p + 1) * SUP)
                    main_ref[0, rows, at] = real
                    main_ref[1, rows, at] = imag
                else:
                    edge_ref[0, :, at] = real
                    edge_ref[1, :, at] = imag
            return carry

        lax.fori_loop(0, blocks, column, 0)

    band = band_ref[0]
    merge(band * blocks, own_ref, own_edge_ref)
    merge((1 - band) * blocks, other_ref, other_edge_ref)


def paint(cells, band, patches):
    main = jax.ShapeDtypeStruct((2, ROWS, NV // 2), jnp.float32)
    edge = jax.ShapeDtypeStruct((2, SUP, NV // 2), jnp.float32)
    smem = pl.BlockSpec(memory_space=pltpu.SMEM)
    vmem = pl.BlockSpec(memory_space=pltpu.VMEM)
    return pl.pallas_call(
        functools.partial(paint_kernel, 16),
        out_shape=(main, edge, main, edge),
        in_specs=[smem, smem, vmem],
        out_specs=(vmem, vmem, vmem, vmem),
        scratch_shapes=[pltpu.VMEM((patches.shape[0] * SUP, LANES), jnp.float32)]
        + [pltpu.VMEM((TILES * HEIGHT, LANES), jnp.float32)] * CHAINS,
        compiler_params=pltpu.CompilerParams(vmem_limit_bytes=56 * 2**20),
        name="paint",
    )(cells, band, patches)


def local(
    visibility,
    plane_index,
    beam_index,
    strip_index,
    cell_row,
    cell_column,
    phase_index,
    kernel_table,
):
    blocks = visibility.shape[0]
    strips = lax.axis_size("tile")
    planes_band, beam_count, phase_local, row_width = kernel_table.shape
    phases = phase_local * strips
    band_index = lax.axis_index("wband")
    strip_capacity = 2 * blocks // strips
    phase_capacity = 2 * blocks // phases * phase_local
    both = phase_capacity + strip_capacity

    owner = phase_index // phase_local
    key = ((plane_index - band_index * planes_band) * beam_count + beam_index) * phase_local
    key = key + phase_index % phase_local
    cell = ((cell_column // STRIDE + 1) * HEIGHT + cell_row) * STRIDE + cell_column % STRIDE

    owner_rank = rank_in_bucket(owner, strips)
    strip_rank = rank_in_bucket(strip_index, strips)
    notes = (
        jnp.zeros((strips * both,), jnp.int32)
        .at[
            jnp.concatenate(
                [owner * both + owner_rank, strip_index * both + phase_capacity + strip_rank]
            )
        ]
        .set(jnp.concatenate([key, cell]), unique_indices=True, mode="drop")
    )
    notes = lax.all_to_all(
        notes.reshape(strips, both), "tile", split_axis=0, concat_axis=0, tiled=True
    )
    keys = notes[:, :phase_capacity].reshape(-1)
    cells = notes[:, phase_capacity:].reshape(-1)

    rows = fetch_rows(keys, kernel_table.reshape(-1, row_width))
    rows = lax.all_to_all(
        rows.reshape(strips, phase_capacity, row_width), "tile", split_axis=0, concat_axis=0, tiled=True
    ).reshape(-1, row_width)
    patches = place_patches(
        owner * phase_capacity + owner_rank,
        strip_index * strip_capacity + strip_rank,
        visibility,
        rows,
        strips * strip_capacity,
    )
    patches = lax.all_to_all(
        patches.reshape(strips, strip_capacity, row_width), "tile", split_axis=0, concat_axis=0, tiled=True
    ).reshape(-1, row_width)

    own, own_edge, other, other_edge = paint(cells, band_index.reshape(1).astype(jnp.int32), patches)
    bands = lax.axis_size("wband")
    received = lax.ppermute(other, "wband", [(b, 1 - b) for b in range(bands)])
    straight = lax.ppermute(own_edge, "tile", [(t, t + 1) for t in range(strips - 1)])
    crossed = lax.ppermute(
        other_edge,
        ("wband", "tile"),
        [(b * strips + t, (1 - b) * strips + t + 1) for b in range(bands) for t in range(strips - 1)],
    )
    edge = jnp.pad(straight + crossed, ((0, 0), (0, ROWS - SUP), (0, 0)))
    return own + received + edge


def solution(mesh):
    placed = (
        P(("groups", "wband", "tile"), None),
        P(("groups", "wband", "tile")),
        P(("groups", "wband", "tile")),
        P(("groups", "wband", "tile")),
        P(("groups", "wband", "tile")),
        P(("groups", "wband", "tile")),
        P(("groups", "wband", "tile")),
        P("wband", None, "tile", None),
    )
    return jax.shard_map(
        local,
        mesh=mesh,
        in_specs=placed,
        out_specs=P(None, ("groups", "tile"), "wband"),
        check_vma=False,
    )
```

time: 1080 us -> 182 us (0.17)
  local copies, waits for them, and re-layouts: 491 us -> 19.3 us
  matrix products: 279 us -> 0 us
  waiting for transfers between devices: 255 us -> 60 us
  Pallas kernels: 0 us -> 64.2 us
  blocking collectives: 0 us -> 13.7 us
  between operations: 13.5 us -> 0.16 us
    convert_element_type x8 -> x0, local copies, waits for them, and re-layouts: 383 us -> none  [add_group(): lifted = jnp.einsum('gti,gkiw->gktw', row_select, placed, preferred_eleme...]
    dot_general x16 -> x0, matrix products: 279 us -> none  [the longest x8 142 us: add_group(): jnp.einsum('gb,gktw->ktbw', block_select, lifted, preferred_element_type=...]
    all_gather x1 -> x0, waiting for transfers between devices: 210 us -> none  [local(): gathered = lax.all_gather(kernel_table, 'tile', axis=2, tiled=True)]
    pallas_call x0 -> x3, Pallas kernels: none -> 64.2 us  [the longest x1 49.8 us: paint(): pl.pallas_call(functools.partial(paint_kernel, 16), out_shape=(main, edge...]
    scatter-add x3 -> x0, local copies, waits for them, and re-layouts: 47.6 us -> none  [the longest x1 41.4 us: paint(): canvas = canvas.at[:, :, 1:, :support].add(totals[..., lanes:])]
    all_to_all x2, waiting for transfers between devices: 25.3 us -> 49.9 us  [the longest x1 25.2 us: local(): lax.all_to_all(patches.reshape(strips, strip_capacity, row_width), 'tile'...]
    unnamed x4 -> x10, local copies, waits for them, and re-layouts: 22.8 us -> 3.19 us
    all_to_all x0 -> x1, blocking collectives: none -> 13.7 us  [local(): lax.all_to_all(notes.reshape(strips, both), 'tile', split_axis=0, concat_...]
  transfers between devices with their start and end apart: 5 -> 5, of which waited for: 4 -> 4; matrix products, arithmetic and copies ran while one was open for 4% -> 0% of each run, Pallas kernels for 0% -> 0%
where the time goes in v1:
time: 182 us; the launch traced here: 181 us
  Pallas kernels  64.2 us (35%)
  waiting for transfers between devices  60 us (33%)
  local copies, waits for them, and re-layouts  19.3 us (11%)
  blocking collectives  13.7 us (8%)
  starting transfers between devices  12.5 us (7%)
  other arithmetic  11.3 us (6%)
    pallas_call x1, Pallas kernels, paint(): pl.pallas_call(functools.partial(paint_kernel, 16), out_shape=(main, edge...  49.8 us
    all_to_all x1, waiting for transfers between devices, local(): lax.all_to_all(patches.reshape(strips, strip_capacity, row_width), 'tile'...  25.2 us
    all_to_all x1, waiting for transfers between devices, local(): lax.all_to_all(rows.reshape(strips, phase_capacity, row_width), 'tile', s...  24.7 us
    scatter x1, local copies, waits for them, and re-layouts, local(): notes = jnp.zeros((strips * both,), jnp.int32).at[jnp.concatenate([owner...  15.5 us
    all_to_all x1, blocking collectives, local(): lax.all_to_all(notes.reshape(strips, both), 'tile', split_axis=0, concat_...  13.7 us
    pallas_call x1, Pallas kernels, place_patches(): pl.pallas_call(functools.partial(patch_kernel, 16), out_shape=jax.ShapeDt...  7.8 us
    pallas_call x1, Pallas kernels, fetch_rows(): pl.pallas_call(functools.partial(fetch_kernel, 16), out_shape=jax.ShapeDt...  6.59 us
    ppermute x1, waiting for transfers between devices, local(): lax.ppermute(other_edge, ('wband', 'tile'), [(b * strips + t, (1 - b) * s...  5.23 us
  transfers between devices with their start and end apart: 5, of which 4 were waited for; matrix products, arithmetic and copies ran while one was open for 0% of the time, Pallas kernels for 0%

profile of v1, /device:TPU:0, one launch (start us, length us, event | category | flops | bytes accessed | tf_op | source)
XLA Modules:
  0.0 181.2 jit_solution(2209157567177387925)
XLA Ops:
  0.0 0.8 fusion.8
  0.8 2.3 %reduce-window.14 = s32[8,16,128]{2,1,0:T(8,128)S(1)} reduce-window(s32[8,16,128]{2,1,0:T(8,128)S(1)} %fusion.4, s32[]{:T(128)} %constant.63.clone.1), window={size=1x1x128 pad=0_0x0_0x127_0}, to_apply=%region_0.1 | reduce-window | flops 2080768 | bytes 131076 | tf_op jit(solution)/shard_map/reduce-window
  3.1 0.3 slice_reduce_fusion.1
  3.4 0.2 reduce-window.15
  3.5 0.1 add_bitcast_fusion.1
  3.7 0.7 fusion.5
  4.4 2.3 %reduce-window.16 = s32[8,16,128]{2,1,0:T(8,128)S(1)} reduce-window(s32[8,16,128]{2,1,0:T(8,128)S(1)} %fusion.5, s32[]{:T(128)} %constant.63.clone.1), window={size=1x1x128 pad=0_0x0_0x127_0}, to_apply=%region_3.4 | reduce-window | flops 2080768 | bytes 131076 | tf_op jit(solution)/shard_map/reduce-window.2
  6.7 0.3 slice_reduce_fusion
  7.0 0.2 reduce-window.19
  7.1 0.1 add_bitcast_fusion
  7.2 0.7 fusion.1
  8.0 0.7 multiply_add_fusion
  8.7 15.5 %scatter_custom_fusion = s32[8192]{0:T(1024)S(1)} fusion(s32[4096]{0:T(1024)S(1)} %bitcast.69, s32[4096]{0:T(1024)S(1)} %pad_add_fusion.1, s32[]{:T(128)} %constant.63.clone.1), kind=kCustom, calls=%fused_computation.23 | custom fusion | bytes 32772 | tf_op jit(solution)/shard_map/scatter | solution.py:236
  24.3 13.7 %all_to_all.22 = s32[8,1,1024]{2,1,0:T(1,128)S(1)} all-to-all(s32[8,1,1024]{2,1,0:T(1,128)S(1)} %bitcast.60), channel_id=1, replica_groups=mesh['groups'=2,'wband'=2,'tile'=8] {'tile'}, dimensions={0} | all-to-all | bytes 65536 | tf_op jit(solution)/shard_map/all_to_all | solution.py:238
  38.0 0.0 copy-start
  38.0 1.6 copy-done
  39.6 0.0 copy-start.2
  39.6 6.6 %fetch_rows.1 = bf16[4096,128]{1,0:T(8,128)(2,1)} custom-call(s32[4096]{0:T(1024)S(1)} %bitcast.56, bf16[8192,128]{1,0:T(8,128)(2,1)S(1)} %bitcast.55), custom_call_target="tpu_custom_call" | custom-call | tf_op jit(solution)/shard_map/fetch_rows/pallas_call | solution.py:43
  46.2 3.6 %all-to-all-start.1 = ((bf16[8,512,128]{2,1,0:T(8,128)(2,1)}), bf16[8,512,128]{2,1,0:T(8,128)(2,1)S(1)}, u32[]{:S(2)}, u32[]{:S(2)}) async-start(bf16[8,512,128]{2,1,0:T(8,128)(2,1)} %bitcast.12), calls=%async_computation.1 | async-start | bytes 2097152 | tf_op jit(solution)/shard_map/all_to_all | solution.py:245
  49.8 0.0 copy-done.2
  49.8 24.7 %all-to-all-done.1 = bf16[8,512,128]{2,1,0:T(8,128)(2,1)S(1)} async-done(((bf16[8,512,128]{2,1,0:T(8,128)(2,1)}), bf16[8,512,128]{2,1,0:T(8,128)(2,1)S(1)}, u32[]{:S(2)}, u32[]{:S(2)}) %all-to-all-start.1) | async-done | bytes 1048608 | tf_op jit(solution)/shard_map/all_to_all | solution.py:245
  74.5 7.8 %place_patches.1 = bf16[4096,128]{1,0:T(8,128)(2,1)} custom-call(s32[2048]{0:T(1024)S(1)} %get-tuple-element.19.source_ref, s32[2048]{0:T(1024)S(1)} %get-tuple-element.17.place_ref, f32[2048]{0:T(1024)S(1)} %bitcast.58, f32[2048]{0:T(1024)S(1)} %bitcast.57, bf16[4096,128]{1,0:T(8,128)(2,1)S(1)} %bitcast.54), custom_call_target="tpu_custom_call" | custom-call | tf_op jit(solution)/shard_map/place_patches/pallas_call | solution.py:85
  82.3 3.6 %all-to-all-start.2 = ((bf16[8,512,128]{2,1,0:T(8,128)(2,1)}), bf16[8,512,128]{2,1,0:T(8,128)(2,1)S(1)}, u32[]{:S(2)}, u32[]{:S(2)}) async-start(bf16[8,512,128]{2,1,0:T(8,128)(2,1)} %bitcast.14), calls=%async_computation.2 | async-start | bytes 2097152 | tf_op jit(solution)/shard_map/all_to_all | solution.py:255
  85.9 0.6 copy.12
  86.5 25.2 %all-to-all-done.2 = bf16[8,512,128]{2,1,0:T(8,128)(2,1)S(1)} async-done(((bf16[8,512,128]{2,1,0:T(8,128)(2,1)}), bf16[8,512,128]{2,1,0:T(8,128)(2,1)S(1)}, u32[]{:S(2)}, u32[]{:S(2)}) %all-to-all-start.2) | async-done | bytes 1048608 | tf_op jit(solution)/shard_map/all_to_all | solution.py:255
  111.7 0.0 copy-start.1
  111.7 1.0 copy-done.1
  112.7 49.8 %paint.1 = (f32[2,64,4096]{2,1,0:T(8,128)}, f32[2,8,4096]{2,1,0:T(8,128)}, f32[2,64,4096]{2,1,0:T(8,128)}, f32[2,8,4096]{2,1,0:T(8,128)}) custom-call(s32[4096]{0:T(1024)} %bitcast.64, s32[1]{0:T(128)} %bitcast.8.band_ref, bf16[4096,128]{1,0:T(8,128)(2,1)} %bitcast.59), custom_call_target="tpu_custom_call" | custom-call | tf_op jit(solution)/shard_map/paint/pallas_call | solution.py:191
  162.5 0.0 collective-permute-start
  162.5 3.3 %collective-permute-start.1 = (f32[2,8,4096]{2,1,0:T(8,128)}, f32[2,8,4096]{2,1,0:T(8,128)S(1)}, u32[]{:S(2)}, u32[]{:S(2)}) collective-permute-start(f32[2,8,4096]{2,1,0:T(8,128)} %get-tuple-element.11), channel_id=1, source_target_pairs={{0,1},{1,2},{2,3},{3,4},{4,5},{5,6},{6,7},{8,9},{9,10},{10,11},{11... | collective-permute-start | bytes 786440 | tf_op jit(solution)/shard_map/ppermute | solution.py:262
  165.8 2.0 %collective-permute-start.2 = (f32[2,8,4096]{2,1,0:T(8,128)}, f32[2,8,4096]{2,1,0:T(8,128)S(1)}, u32[]{:S(2)}, u32[]{:S(2)}) collective-permute-start(f32[2,8,4096]{2,1,0:T(8,128)} %get-tuple-element.12), channel_id=1, source_target_pairs={{0,9},{1,10},{2,11},{3,12},{4,13},{5,14},{6,15},{8,1},{9,2},{10,3}... | collective-permute-start | bytes 786440 | tf_op jit(solution)/shard_map/ppermute | solution.py:263
  167.8 4.9 %collective-permute-done.1 = f32[2,8,4096]{2,1,0:T(8,128)S(1)} collective-permute-done((f32[2,8,4096]{2,1,0:T(8,128)}, f32[2,8,4096]{2,1,0:T(8,128)S(1)}, u32[]{:S(2)}, u32[]{:S(2)}) %collective-permute-start.1) | collective-permute-done | bytes 262176 | tf_op jit(solution)/shard_map/ppermute | solution.py:262
  172.7 5.2 %collective-permute-done.2 = f32[2,8,4096]{2,1,0:T(8,128)S(1)} collective-permute-done((f32[2,8,4096]{2,1,0:T(8,128)}, f32[2,8,4096]{2,1,0:T(8,128)S(1)}, u32[]{:S(2)}, u32[]{:S(2)}) %collective-permute-start.2) | collective-permute-done | bytes 262176 | tf_op jit(solution)/shard_map/ppermute | solution.py:263
  177.9 0.0 collective-permute-done
  177.9 3.2 %pad_add_fusion = f32[2,64,4096]{2,1,0:T(8,128)} fusion(f32[2,8,4096]{2,1,0:T(8,128)S(1)} %add.88, f32[2,64,4096]{2,1,0:T(8,128)} %get-tuple-element.9, f32[2,64,4096]{2,1,0:T(8,128)S(1)} %collective-permute-done), kind=kLoop, calls=%fused_computation.1 | loop fusion | flops 1048576 | bytes 6553600 | tf_op jit(solution)/shard_map/add | solution.py:269
  (10 shorter events, 0.1 us)
Async XLA Ops:
  38.0 1.6 copy-start
  39.6 10.2 %copy-start.2 = (f32[2048,2]{0,1:T(2,128)S(1)}, f32[2048,2]{0,1:T(2,128)}, u32[]{:S(2)}) copy-start(f32[2048,2]{0,1:T(2,128)} %param.8) | copy-start | bytes 49156
  46.2 28.3 %all-to-all-start.1 = ((bf16[8,512,128]{2,1,0:T(8,128)(2,1)}), bf16[8,512,128]{2,1,0:T(8,128)(2,1)S(1)}, u32[]{:S(2)}, u32[]{:S(2)}) async-start(bf16[8,512,128]{2,1,0:T(8,128)(2,1)} %bitcast.12), calls=%async_computation.1 | async-start | bytes 2097152 | tf_op jit(solution)/shard_map/all_to_all | solution.py:245
  82.3 29.4 %all-to-all-start.2 = ((bf16[8,512,128]{2,1,0:T(8,128)(2,1)}), bf16[8,512,128]{2,1,0:T(8,128)(2,1)S(1)}, u32[]{:S(2)}, u32[]{:S(2)}) async-start(bf16[8,512,128]{2,1,0:T(8,128)(2,1)} %bitcast.14), calls=%async_computation.2 | async-start | bytes 2097152 | tf_op jit(solution)/shard_map/all_to_all | solution.py:255
  111.7 1.0 copy-start.1
  162.5 15.5 %collective-permute-start = (f32[2,64,4096]{2,1,0:T(8,128)}, f32[2,64,4096]{2,1,0:T(8,128)S(1)}, u32[]{:S(2)}, u32[]{:S(2)}) collective-permute-start(f32[2,64,4096]{2,1,0:T(8,128)} %get-tuple-element.10), channel_id=1, source_target_pairs={{0,8},{8,0},{1,9},{9,1},{2,10},{10,2},{3,11},{11,3},{4,12},{12,4},... | collective-permute-start | bytes 6291464 | tf_op jit(solution)/shard_map/ppermute | solution.py:261
  162.5 10.2 %collective-permute-start.1 = (f32[2,8,4096]{2,1,0:T(8,128)}, f32[2,8,4096]{2,1,0:T(8,128)S(1)}, u32[]{:S(2)}, u32[]{:S(2)}) collective-permute-start(f32[2,8,4096]{2,1,0:T(8,128)} %get-tuple-element.11), channel_id=1, source_target_pairs={{0,1},{1,2},{2,3},{3,4},{4,5},{5,6},{6,7},{8,9},{9,10},{10,11},{11... | collective-permute-start | bytes 786440 | tf_op jit(solution)/shard_map/ppermute | solution.py:262
  165.8 12.1 %collective-permute-start.2 = (f32[2,8,4096]{2,1,0:T(8,128)}, f32[2,8,4096]{2,1,0:T(8,128)S(1)}, u32[]{:S(2)}, u32[]{:S(2)}) collective-permute-start(f32[2,8,4096]{2,1,0:T(8,128)} %get-tuple-element.12), channel_id=1, source_target_pairs={{0,9},{1,10},{2,11},{3,12},{4,13},{5,14},{6,15},{8,1},{9,2},{10,3}... | collective-permute-start | bytes 786440 | tf_op jit(solution)/shard_map/ppermute | solution.py:263

commit v2 on v1

--- a/solution.py
+++ b/solution.py
@@ -20,9 +20,89 @@
 
 
 def rank_in_bucket(target, buckets):
-    onehot = (target[:, None] == jnp.arange(buckets, dtype=jnp.int32)[None, :]).astype(jnp.int32)
-    ranking = jnp.cumsum(onehot, axis=0) - 1
-    return jnp.sum(ranking * onehot, axis=1)
+    rows = target.shape[0]
+    bucket = lax.broadcasted_iota(jnp.int32, (buckets, rows, LANES), 0)
+    member = jnp.where(target[None] == bucket, 1.0, 0.0).reshape(buckets * rows, LANES)
+    member = member.astype(jnp.bfloat16)
+    up = lax.broadcasted_iota(jnp.int32, (LANES, LANES), 0)
+    down = lax.broadcasted_iota(jnp.int32, (LANES, LANES), 1)
+    within = jnp.dot(
+        member, jnp.where(up < down, 1.0, 0.0).astype(jnp.bfloat16), preferred_element_type=jnp.float32
+    )
+    totals = jnp.dot(
+        member, jnp.ones((LANES, LANES), jnp.bfloat16), preferred_element_type=jnp.float32
+    )
+    count = buckets * rows
+    left = lax.broadcasted_iota(jnp.int32, (count, count), 0)
+    right = lax.broadcasted_iota(jnp.int32, (count, count), 1)
+    earlier = jnp.where((right < left) & (right // rows == left // rows), 1.0, 0.0)
+    above = jnp.dot(
+        earlier.astype(jnp.bfloat16), totals.astype(jnp.bfloat16), preferred_element_type=jnp.float32
+    )
+    ranks = member.astype(jnp.float32) * (within + above)
+    return jnp.sum(ranks.reshape(buckets, rows, LANES), axis=0).astype(jnp.int32)
+
+
+def address_kernel(
+    sizes, band_ref, plane_ref, beam_ref, strip_ref, row_ref, column_ref, phase_ref,
+    key_ref, cell_ref, source_ref, place_ref, key_at_ref, cell_at_ref,
+):
+    strips, planes_band, beam_count, phase_local, phase_capacity, strip_capacity = sizes
+    both = phase_capacity + strip_capacity
+    phase, strip, column = phase_ref[...], strip_ref[...], column_ref[...]
+    owner = phase // phase_local
+    key = ((plane_ref[...] - band_ref[0] * planes_band) * beam_count + beam_ref[...]) * phase_local
+    key_ref[...] = key + (phase - owner * phase_local)
+    tile_row = ((column >> SHIFT) + 1) * HEIGHT + row_ref[...]
+    cell_ref[...] = tile_row * STRIDE + (column & (STRIDE - 1))
+    owner_rank = rank_in_bucket(owner, strips)
+    strip_rank = rank_in_bucket(strip, strips)
+    source_ref[...] = owner * phase_capacity + owner_rank
+    place_ref[...] = strip * strip_capacity + strip_rank
+    key_at_ref[...] = owner * both + owner_rank
+    cell_at_ref[...] = strip * both + phase_capacity + strip_rank
+
+
+def addresses(sizes, band, *columns):
+    blocks = columns[0].shape[0]
+    shape = jax.ShapeDtypeStruct((blocks // LANES, LANES), jnp.int32)
+    vmem = pl.BlockSpec(memory_space=pltpu.VMEM)
+    results = pl.pallas_call(
+        functools.partial(address_kernel, sizes),
+        out_shape=(shape,) * 6,
+        in_specs=[pl.BlockSpec(memory_space=pltpu.SMEM)] + [vmem] * len(columns),
+        out_specs=(vmem,) * 6,
+        compiler_params=pltpu.CompilerParams(vmem_limit_bytes=40 * 2**20),
+        name="addresses",
+    )(band, *(column.reshape(shape.shape) for column in columns))
+    return [result.reshape(blocks) for result in results]
+
+
+def notes_kernel(unroll, key_ref, cell_ref, key_at_ref, cell_at_ref, blank_ref, out_ref, sem):
+    copy = pltpu.make_async_copy(blank_ref, out_ref, sem)
+    copy.start()
+    copy.wait()
+
+    def body(i, carry):
+        for u in range(unroll):
+            n = i * unroll + u
+            out_ref[key_at_ref[n]] = key_ref[n]
+            out_ref[cell_at_ref[n]] = cell_ref[n]
+        return carry
+
+    lax.fori_loop(0, key_ref.shape[0] // unroll, body, 0)
+
+
+def write_notes(key, cell, key_at, cell_at, total):
+    smem = pl.BlockSpec(memory_space=pltpu.SMEM)
+    return pl.pallas_call(
+        functools.partial(notes_kernel, 16),
+        out_shape=jax.ShapeDtypeStruct((total,), jnp.int32),
+        in_specs=[smem] * 4 + [pl.BlockSpec(memory_space=pl.ANY)],
+        out_specs=smem,
+        scratch_shapes=[pltpu.SemaphoreType.DMA],
+        name="write_notes",
+    )(key, cell, key_at, cell_at, jnp.zeros((total,), jnp.int32))
 
 
 def fetch_kernel(unroll, keys_ref, table_ref, out_ref, wide, picked):
@@ -127,19 +207,28 @@
 
     lane = lax.broadcasted_iota(jnp.int32, (SUP, LANES), 1)
 
-    def body(i, carry):
+    def moved_group(i):
         spread = []
         for u in range(unroll):
             n = i * unroll + u
-            cell = cells_ref[n]
             patch = wide[pl.ds(pl.multiple_of(n * SUP, SUP), SUP), :]
-            spread.append((cell >> SHIFT, pltpu.roll(patch, cell & (STRIDE - 1), 1)))
-        for u, (start, moved) in enumerate(spread):
+            spread.append(pltpu.roll(patch, cells_ref[n] & (STRIDE - 1), 1))
+        return tuple(spread)
+
+    def add_group(i, spread):
+        for u, moved in enumerate(spread):
+            start = cells_ref[i * unroll + u] >> SHIFT
             canvas = canvases[u % len(canvases)]
             canvas[pl.ds(start, SUP), :] = canvas[pl.ds(start, SUP), :] + moved
-        return carry
-
-    lax.fori_loop(0, patches_ref.shape[0] // unroll, body, 0)
+
+    def body(i, spread):
+        following = moved_group(i + 1)
+        add_group(i, spread)
+        return following
+
+    groups = patches_ref.shape[0] // unroll
+    last = lax.fori_loop(0, groups - 1, body, moved_group(0))
+    add_group(groups - 1, last)
 
     per_block = LANES // STRIDE
     blocks = NV // LANES // 2
@@ -189,7 +278,7 @@
     smem = pl.BlockSpec(memory_space=pltpu.SMEM)
     vmem = pl.BlockSpec(memory_space=pltpu.VMEM)
     return pl.pallas_call(
-        functools.partial(paint_kernel, 16),
+        functools.partial(paint_kernel, 64),
         out_shape=(main, edge, main, edge),
         in_specs=[smem, smem, vmem],
         out_specs=(vmem, vmem, vmem, vmem),
@@ -219,22 +308,12 @@
     phase_capacity = 2 * blocks // phases * phase_local
     both = phase_capacity + strip_capacity
 
-    owner = phase_index // phase_local
-    key = ((plane_index - band_index * planes_band) * beam_count + beam_index) * phase_local
-    key = key + phase_index % phase_local
-    cell = ((cell_column // STRIDE + 1) * HEIGHT + cell_row) * STRIDE + cell_column % STRIDE
-
-    owner_rank = rank_in_bucket(owner, strips)
-    strip_rank = rank_in_bucket(strip_index, strips)
-    notes = (
-        jnp.zeros((strips * both,), jnp.int32)
-        .at[
-            jnp.concatenate(
-                [owner * both + owner_rank, strip_index * both + phase_capacity + strip_rank]
-            )
-        ]
-        .set(jnp.concatenate([key, cell]), unique_indices=True, mode="drop")
-    )
+    band = band_index.reshape(1).astype(jnp.int32)
+    sizes = (strips, planes_band, beam_count, phase_local, phase_capacity, strip_capacity)
+    key, cell, source, place, key_at, cell_at = addresses(
+        sizes, band, plane_index, beam_index, strip_index, cell_row, cell_column, phase_index
+    )
+    notes = write_notes(key, cell, key_at, cell_at, strips * both)
     notes = lax.all_to_all(
         notes.reshape(strips, both), "tile", split_axis=0, concat_axis=0, tiled=True
     )
@@ -246,8 +325,8 @@
         rows.reshape(strips, phase_capacity, row_width), "tile", split_axis=0, concat_axis=0, tiled=True
     ).reshape(-1, row_width)
     patches = place_patches(
-        owner * phase_capacity + owner_rank,
-        strip_index * strip_capacity + strip_rank,
+        source,
+        place,
         visibility,
         rows,
         strips * strip_capacity,
@@ -256,7 +335,7 @@
         patches.reshape(strips, strip_capacity, row_width), "tile", split_axis=0, concat_axis=0, tiled=True
     ).reshape(-1, row_width)
 
-    own, own_edge, other, other_edge = paint(cells, band_index.reshape(1).astype(jnp.int32), patches)
+    own, own_edge, other, other_edge = paint(cells, band, patches)
     bands = lax.axis_size("wband")
     received = lax.ppermute(other, "wband", [(b, 1 - b) for b in range(bands)])
     straight = lax.ppermute(own_edge, "tile", [(t, t + 1) for t in range(strips - 1)])

time: 182 us -> 162 us (0.89)
  local copies, waits for them, and re-layouts: 19.3 us -> 10.4 us
  other arithmetic: 11.3 us -> 3.27 us
  Pallas kernels: 64.2 us -> 60.7 us
    scatter x1 -> x0, local copies, waits for them, and re-layouts: 15.5 us -> none  [local(): notes = jnp.zeros((strips * both,), jnp.int32).at[jnp.concatenate([owner...]
    unnamed x10 -> x30, local copies, waits for them, and re-layouts: 3.19 us -> 9.73 us
    another operation x4 -> x0, other arithmetic: 4.87 us -> none
    pallas_call x1 -> x3, Pallas kernels: 49.8 us -> 46.3 us  [the longest x1 35.8 us: paint(): pl.pallas_call(functools.partial(paint_kernel, 64), out_shape=(main, edge...]
where the time goes in v2:
time: 162 us; the launch traced here: 161 us
  Pallas kernels  60.7 us (37%)
  waiting for transfers between devices  60 us (37%)
  blocking collectives  13.9 us (9%)
  starting transfers between devices  12.5 us (8%)
  local copies, waits for them, and re-layouts  10.4 us (6%)
  other arithmetic  3.27 us (2%)
    pallas_call x1, Pallas kernels, paint(): pl.pallas_call(functools.partial(paint_kernel, 64), out_shape=(main, edge...  35.8 us
    all_to_all x1, waiting for transfers between devices, local(): lax.all_to_all(patches.reshape(strips, strip_capacity, row_width), 'tile'...  25.2 us
    all_to_all x1, waiting for transfers between devices, local(): lax.all_to_all(rows.reshape(strips, phase_capacity, row_width), 'tile', s...  24.7 us
    all_to_all x1, blocking collectives, local(): lax.all_to_all(notes.reshape(strips, both), 'tile', split_axis=0, concat_...  13.9 us
    pallas_call x1, Pallas kernels, write_notes(): pl.pallas_call(functools.partial(notes_kernel, 16), out_shape=jax.ShapeDt...  10.2 us
    unnamed x30, local copies, waits for them, and re-layouts  9.73 us
    pallas_call x1, Pallas kernels, place_patches(): pl.pallas_call(functools.partial(patch_kernel, 16), out_shape=jax.ShapeDt...  7.8 us
    pallas_call x1, Pallas kernels, fetch_rows(): pl.pallas_call(functools.partial(fetch_kernel, 16), out_shape=jax.ShapeDt...  6.59 us
  transfers between devices with their start and end apart: 5, of which 4 were waited for; matrix products, arithmetic and copies ran while one was open for 0% of the time, Pallas kernels for 0%

profile of v2, /device:TPU:0, one launch (start us, length us, event | category | flops | bytes accessed | tf_op | source)
XLA Modules:
  0.0 160.9 jit_solution(15385129871701044752)
XLA Ops:
  0.0 0.0 copy-start.1
  0.0 0.7 copy-done.1
  0.7 0.0 copy-start.2
  0.7 0.7 copy-done.2
  1.4 0.0 copy-start.3
  1.4 0.7 copy-done.3
  2.1 0.0 copy-start.4
  2.1 0.7 copy-done.4
  2.8 0.0 copy-start.5
  2.8 0.7 copy-done.5
  3.5 0.0 copy-start.6
  3.5 0.7 copy-done.6
  4.2 0.3 addresses.1
  4.5 0.0 copy-start.7
  4.5 0.6 copy-done.7
  5.1 0.0 copy-start.8
  5.1 0.6 copy-done.8
  5.7 0.0 copy-start.9
  5.7 0.6 copy-done.9
  6.3 0.0 copy-start.10
  6.3 0.6 copy-done.10
  6.9 0.6 broadcast_in_dim.3.blank_ref
  7.5 10.2 %write_notes.1 = s32[8192]{0:T(1024)} custom-call(s32[2048]{0:T(1024)} %bitcast.43, s32[2048]{0:T(1024)} %bitcast.44, s32[2048]{0:T(1024)} %bitcast.45, s32[2048]{0:T(1024)} %bitcast.46, s32[8192]{0:T(1024)} %broadcast_in_dim.3.blank_ref), custom_call_target="tpu_custom_call" | custom-call | tf_op jit(solution)/shard_map/write_notes/pallas_call | solution.py:98
  17.7 13.9 %all_to_all.22 = s32[8,1,1024]{2,1,0:T(1,128)S(1)} all-to-all(s32[8,1,1024]{2,1,0:T(1,128)} %bitcast.48), channel_id=1, replica_groups=mesh['groups'=2,'wband'=2,'tile'=8] {'tile'}, dimensions={0} | all-to-all | bytes 65536 | tf_op jit(solution)/shard_map/all_to_all | solution.py:317
  31.7 0.0 copy-start
  31.7 1.6 copy-done
  33.3 0.0 copy-start.12
  33.3 6.6 %fetch_rows.1 = bf16[4096,128]{1,0:T(8,128)(2,1)} custom-call(s32[4096]{0:T(1024)S(1)} %bitcast.32, bf16[8192,128]{1,0:T(8,128)(2,1)S(1)} %bitcast.31), custom_call_target="tpu_custom_call" | custom-call | tf_op jit(solution)/shard_map/fetch_rows/pallas_call | solution.py:123
  39.9 3.6 %all-to-all-start.1 = ((bf16[8,512,128]{2,1,0:T(8,128)(2,1)}), bf16[8,512,128]{2,1,0:T(8,128)(2,1)S(1)}, u32[]{:S(2)}, u32[]{:S(2)}) async-start(bf16[8,512,128]{2,1,0:T(8,128)(2,1)} %bitcast.17), calls=%async_computation.1 | async-start | bytes 2097152 | tf_op jit(solution)/shard_map/all_to_all | solution.py:324
  43.4 0.0 copy-done.12
  43.5 24.7 %all-to-all-done.1 = bf16[8,512,128]{2,1,0:T(8,128)(2,1)S(1)} async-done(((bf16[8,512,128]{2,1,0:T(8,128)(2,1)}), bf16[8,512,128]{2,1,0:T(8,128)(2,1)S(1)}, u32[]{:S(2)}, u32[]{:S(2)}) %all-to-all-start.1) | async-done | bytes 1048608 | tf_op jit(solution)/shard_map/all_to_all | solution.py:324
  68.2 7.8 %place_patches.1 = bf16[4096,128]{1,0:T(8,128)(2,1)} custom-call(s32[2048]{0:T(1024)S(1)} %bitcast.35, s32[2048]{0:T(1024)S(1)} %bitcast.36, f32[2048]{0:T(1024)S(1)} %bitcast.34, f32[2048]{0:T(1024)S(1)} %bitcast.33, bf16[4096,128]{1,0:T(8,128)(2,1)S(1)} %bitcast.30), custom_call_target="tpu_custom_call" | custom-call | tf_op jit(solution)/shard_map/place_patches/pallas_call | solution.py:165
  76.0 3.6 %all-to-all-start.2 = ((bf16[8,512,128]{2,1,0:T(8,128)(2,1)}), bf16[8,512,128]{2,1,0:T(8,128)(2,1)S(1)}, u32[]{:S(2)}, u32[]{:S(2)}) async-start(bf16[8,512,128]{2,1,0:T(8,128)(2,1)} %bitcast.19), calls=%async_computation.2 | async-start | bytes 2097152 | tf_op jit(solution)/shard_map/all_to_all | solution.py:334
  79.5 0.6 copy.10
  80.1 25.2 %all-to-all-done.2 = bf16[8,512,128]{2,1,0:T(8,128)(2,1)S(1)} async-done(((bf16[8,512,128]{2,1,0:T(8,128)(2,1)}), bf16[8,512,128]{2,1,0:T(8,128)(2,1)S(1)}, u32[]{:S(2)}, u32[]{:S(2)}) %all-to-all-start.2) | async-done | bytes 1048608 | tf_op jit(solution)/shard_map/all_to_all | solution.py:334
  105.3 0.0 copy-start.11
  105.3 1.0 copy-done.11
  106.3 35.8 %paint.1 = (f32[2,64,4096]{2,1,0:T(8,128)}, f32[2,8,4096]{2,1,0:T(8,128)}, f32[2,64,4096]{2,1,0:T(8,128)}, f32[2,8,4096]{2,1,0:T(8,128)}) custom-call(s32[4096]{0:T(1024)} %bitcast.50, s32[1]{0:T(128)} %bitcast.band_ref, bf16[4096,128]{1,0:T(8,128)(2,1)} %bitcast.47), custom_call_target="tpu_custom_call" | custom-call | tf_op jit(solution)/shard_map/paint/pallas_call | solution.py:280
  142.1 0.0 collective-permute-start
  142.1 3.3 %collective-permute-start.1 = (f32[2,8,4096]{2,1,0:T(8,128)}, f32[2,8,4096]{2,1,0:T(8,128)S(1)}, u32[]{:S(2)}, u32[]{:S(2)}) collective-permute-start(f32[2,8,4096]{2,1,0:T(8,128)} %get-tuple-element.23), channel_id=1, source_target_pairs={{0,1},{1,2},{2,3},{3,4},{4,5},{5,6},{6,7},{8,9},{9,10},{10,11},{11... | collective-permute-start | bytes 786440 | tf_op jit(solution)/shard_map/ppermute | solution.py:341
  145.4 2.0 %collective-permute-start.2 = (f32[2,8,4096]{2,1,0:T(8,128)}, f32[2,8,4096]{2,1,0:T(8,128)S(1)}, u32[]{:S(2)}, u32[]{:S(2)}) collective-permute-start(f32[2,8,4096]{2,1,0:T(8,128)} %get-tuple-element.24), channel_id=1, source_target_pairs={{0,9},{1,10},{2,11},{3,12},{4,13},{5,14},{6,15},{8,1},{9,2},{10,3}... | collective-permute-start | bytes 786440 | tf_op jit(solution)/shard_map/ppermute | solution.py:342
  147.5 4.9 %collective-permute-done.1 = f32[2,8,4096]{2,1,0:T(8,128)S(1)} collective-permute-done((f32[2,8,4096]{2,1,0:T(8,128)}, f32[2,8,4096]{2,1,0:T(8,128)S(1)}, u32[]{:S(2)}, u32[]{:S(2)}) %collective-permute-start.1) | collective-permute-done | bytes 262176 | tf_op jit(solution)/shard_map/ppermute | solution.py:341
  152.3 5.2 %collective-permute-done.2 = f32[2,8,4096]{2,1,0:T(8,128)S(1)} collective-permute-done((f32[2,8,4096]{2,1,0:T(8,128)}, f32[2,8,4096]{2,1,0:T(8,128)S(1)}, u32[]{:S(2)}, u32[]{:S(2)}) %collective-permute-start.2) | collective-permute-done | bytes 262176 | tf_op jit(solution)/shard_map/ppermute | solution.py:342
  157.6 0.0 collective-permute-done
  157.6 3.2 %pad_add_fusion = f32[2,64,4096]{2,1,0:T(8,128)} fusion(f32[2,8,4096]{2,1,0:T(8,128)S(1)} %add.12, f32[2,64,4096]{2,1,0:T(8,128)} %get-tuple-element.21, f32[2,64,4096]{2,1,0:T(8,128)S(1)} %collective-permute-done), kind=kLoop, calls=%fused_computation | loop fusion | flops 1048576 | bytes 6553600 | tf_op jit(solution)/shard_map/add | solution.py:348
  (5 shorter events, 0.1 us)
Async XLA Ops:
  0.0 0.7 copy-start.1
  0.7 0.7 copy-start.2
  1.4 0.7 copy-start.3
  2.1 0.7 copy-start.4
  2.8 0.7 copy-start.5
  3.5 0.7 copy-start.6
  4.5 0.6 copy-start.7
  5.1 0.6 copy-start.8
  5.7 0.6 copy-start.9
  6.3 0.6 copy-start.10
  31.7 1.6 copy-start
  33.3 10.2 %copy-start.12 = (f32[2048,2]{0,1:T(2,128)S(1)}, f32[2048,2]{0,1:T(2,128)}, u32[]{:S(2)}) copy-start(f32[2048,2]{0,1:T(2,128)} %param.8) | copy-start | bytes 49156
  39.9 28.3 %all-to-all-start.1 = ((bf16[8,512,128]{2,1,0:T(8,128)(2,1)}), bf16[8,512,128]{2,1,0:T(8,128)(2,1)S(1)}, u32[]{:S(2)}, u32[]{:S(2)}) async-start(bf16[8,512,128]{2,1,0:T(8,128)(2,1)} %bitcast.17), calls=%async_computation.1 | async-start | bytes 2097152 | tf_op jit(solution)/shard_map/all_to_all | solution.py:324
  76.0 29.4 %all-to-all-start.2 = ((bf16[8,512,128]{2,1,0:T(8,128)(2,1)}), bf16[8,512,128]{2,1,0:T(8,128)(2,1)S(1)}, u32[]{:S(2)}, u32[]{:S(2)}) async-start(bf16[8,512,128]{2,1,0:T(8,128)(2,1)} %bitcast.19), calls=%async_computation.2 | async-start | bytes 2097152 | tf_op jit(solution)/shard_map/all_to_all | solution.py:334
  105.3 1.0 copy-start.11
  142.1 15.5 %collective-permute-start = (f32[2,64,4096]{2,1,0:T(8,128)}, f32[2,64,4096]{2,1,0:T(8,128)S(1)}, u32[]{:S(2)}, u32[]{:S(2)}) collective-permute-start(f32[2,64,4096]{2,1,0:T(8,128)} %get-tuple-element.22), channel_id=1, source_target_pairs={{0,8},{8,0},{1,9},{9,1},{2,10},{10,2},{3,11},{11,3},{4,12},{12,4},... | collective-permute-start | bytes 6291464 | tf_op jit(solution)/shard_map/ppermute | solution.py:340
  142.1 10.2 %collective-permute-start.1 = (f32[2,8,4096]{2,1,0:T(8,128)}, f32[2,8,4096]{2,1,0:T(8,128)S(1)}, u32[]{:S(2)}, u32[]{:S(2)}) collective-permute-start(f32[2,8,4096]{2,1,0:T(8,128)} %get-tuple-element.23), channel_id=1, source_target_pairs={{0,1},{1,2},{2,3},{3,4},{4,5},{5,6},{6,7},{8,9},{9,10},{10,11},{11... | collective-permute-start | bytes 786440 | tf_op jit(solution)/shard_map/ppermute | solution.py:341
  145.4 12.1 %collective-permute-start.2 = (f32[2,8,4096]{2,1,0:T(8,128)}, f32[2,8,4096]{2,1,0:T(8,128)S(1)}, u32[]{:S(2)}, u32[]{:S(2)}) collective-permute-start(f32[2,8,4096]{2,1,0:T(8,128)} %get-tuple-element.24), channel_id=1, source_target_pairs={{0,9},{1,10},{2,11},{3,12},{4,13},{5,14},{6,15},{8,1},{9,2},{10,3}... | collective-permute-start | bytes 786440 | tf_op jit(solution)/shard_map/ppermute | solution.py:342

commit v3 on v2

--- a/solution.py
+++ b/solution.py
@@ -17,6 +17,7 @@
 HEIGHT = ROWS + SUP
 TILES = NV // STRIDE + 1
 CHAINS = 2
+MESH = pl.DeviceIdType.MESH
 
 
 def rank_in_bucket(target, buckets):
@@ -105,36 +106,187 @@
     )(key, cell, key_at, cell_at, jnp.zeros((total,), jnp.int32))
 
 
-def fetch_kernel(unroll, keys_ref, table_ref, out_ref, wide, picked):
+def peer(me, step, count):
+    return lax.rem(me + step + count, count)
+
+
+def greet(devices):
+    barrier = pltpu.get_barrier_semaphore()
+    for device in devices:
+        pl.semaphore_signal(barrier, inc=1, device_id=device, device_id_type=MESH)
+    return barrier
+
+
+def greet_tiles(me, tiles):
+    barrier = pltpu.get_barrier_semaphore()
+
+    def body(step, carry):
+        pl.semaphore_signal(
+            barrier, inc=1, device_id={"tile": peer(me, step, tiles)}, device_id_type=MESH
+        )
+        return carry
+
+    lax.fori_loop(1, tiles, body, 0)
+    return barrier
+
+
+def answer_kernel(
+    tiles, capacity, unroll, notes_ref, table_ref, got_ref, rows_ref,
+    wide, picked, outgoing, listed, note_send, note_recv, row_send, row_recv, own_sem,
+):
+    me = lax.axis_index("tile")
+    barrier = greet_tiles(me, tiles)
     wide[...] = table_ref[...].astype(jnp.float32)
-
-    def body(i, carry):
-        for u in range(unroll):
-            n = i * unroll + u
-            picked[pl.ds(n, 1), :] = wide[pl.ds(keys_ref[n], 1), :]
-        return carry
-
-    lax.fori_loop(0, out_ref.shape[0] // unroll, body, 0)
-    out_ref[...] = picked[...].astype(jnp.bfloat16)
-
-
-def fetch_rows(keys, table):
-    total, width = keys.shape[0], table.shape[1]
+    pl.semaphore_wait(barrier, tiles - 1)
+
+    def note_copy(step, sender):
+        target = peer(me, step, tiles)
+        return pltpu.make_async_remote_copy(
+            src_ref=notes_ref.at[target],
+            dst_ref=got_ref.at[sender],
+            send_sem=note_send.at[step],
+            recv_sem=note_recv.at[step],
+            device_id={"tile": target},
+            device_id_type=MESH,
+        )
+
+    def row_copy(step, sender):
+        target = peer(me, step, tiles)
+        return pltpu.make_async_remote_copy(
+            src_ref=outgoing.at[target],
+            dst_ref=rows_ref.at[sender],
+            send_sem=row_send.at[step],
+            recv_sem=row_recv.at[step],
+            device_id={"tile": target},
+            device_id_type=MESH,
+        )
+
+    def start_notes(step, carry):
+        note_copy(step, me).start()
+        return carry
+
+    def wait_notes(step, carry):
+        note_copy(step, peer(me, -step, tiles)).wait_recv()
+        return carry
+
+    lax.fori_loop(1, tiles, start_notes, 0)
+    got_ref[me] = notes_ref[me]
+    lax.fori_loop(1, tiles, wait_notes, 0)
+    listing = pltpu.make_async_copy(got_ref, listed, own_sem)
+    listing.start()
+    listing.wait()
+
+    def look_up(target):
+        def body(i, carry):
+            for u in range(unroll):
+                j = i * unroll + u
+                key = listed[target, j // LANES, j % LANES]
+                picked[pl.ds(j, 1), :] = wide[pl.ds(key, 1), :]
+            return carry
+
+        lax.fori_loop(0, capacity // unroll, body, 0)
+        outgoing[target] = picked[...].astype(jnp.bfloat16)
+
+    def send_rows(step, carry):
+        look_up(peer(me, step, tiles))
+        row_copy(step, me).start()
+        return carry
+
+    lax.fori_loop(1, tiles, send_rows, 0)
+    look_up(me)
+    keep = pltpu.make_async_copy(outgoing.at[me], rows_ref.at[me], own_sem)
+    keep.start()
+
+    def finish(step, carry):
+        sender = peer(me, -step, tiles)
+        note_copy(step, sender).wait_send()
+        row_copy(step, sender).wait()
+        return carry
+
+    lax.fori_loop(1, tiles, finish, 0)
+    keep.wait()
+
+
+def answer_requests(notes, table, tiles, capacity):
+    width = table.shape[1]
+    notes = notes.reshape(tiles, -1, LANES)
+    vmem = pl.BlockSpec(memory_space=pltpu.VMEM)
     return pl.pallas_call(
-        functools.partial(fetch_kernel, 16),
-        out_shape=jax.ShapeDtypeStruct((total, width), jnp.bfloat16),
-        in_specs=[
-            pl.BlockSpec(memory_space=pltpu.SMEM),
-            pl.BlockSpec(memory_space=pltpu.VMEM),
-        ],
-        out_specs=pl.BlockSpec(memory_space=pltpu.VMEM),
+        functools.partial(answer_kernel, tiles, capacity, 16),
+        out_shape=(
+            jax.ShapeDtypeStruct(notes.shape, jnp.int32),
+            jax.ShapeDtypeStruct((tiles, capacity, width), jnp.bfloat16),
+        ),
+        in_specs=[vmem, vmem],
+        out_specs=(vmem, pl.BlockSpec(memory_space=pl.ANY)),
         scratch_shapes=[
             pltpu.VMEM(table.shape, jnp.float32),
-            pltpu.VMEM((total, width), jnp.float32),
+            pltpu.VMEM((capacity, width), jnp.float32),
+            pltpu.VMEM((tiles, capacity, width), jnp.bfloat16),
+            pltpu.SMEM(notes.shape, jnp.int32),
+            pltpu.SemaphoreType.DMA((tiles,)),
+            pltpu.SemaphoreType.DMA((tiles,)),
+            pltpu.SemaphoreType.DMA((tiles,)),
+            pltpu.SemaphoreType.DMA((tiles,)),
+            pltpu.SemaphoreType.DMA,
         ],
-        compiler_params=pltpu.CompilerParams(vmem_limit_bytes=40 * 2**20),
-        name="fetch_rows",
-    )(keys, table)
+        compiler_params=pltpu.CompilerParams(
+            collective_id=0, has_side_effects=True, vmem_limit_bytes=40 * 2**20
+        ),
+        name="answer_requests",
+    )(notes, table)
+
+
+def edges_kernel(
+    tiles, pieces, other_ref, own_edge_ref, other_edge_ref, got_ref, straight_ref, crossed_ref, sends, recvs
+):
+    me, band = lax.axis_index("tile"), lax.axis_index("wband")
+    after, before = peer(me, 1, tiles), peer(me, -1, tiles)
+    partner = {"wband": 1 - band}
+    barrier = greet(
+        [partner]
+        + [{"wband": side, "tile": tile} for side in (band, 1 - band) for tile in (after, before)]
+    )
+    pl.semaphore_wait(barrier, 5)
+    routes = [(own_edge_ref, straight_ref, {"tile": after})]
+    routes.append((other_edge_ref, crossed_ref, {"wband": 1 - band, "tile": after}))
+    rows = ROWS // pieces
+    for component in range(2):
+        for piece in range(pieces):
+            part = (component, pl.ds(piece * rows, rows))
+            routes.append((other_ref.at[part], got_ref.at[part], partner))
+    copies = [
+        pltpu.make_async_remote_copy(
+            src_ref=source,
+            dst_ref=target,
+            send_sem=sends.at[n],
+            recv_sem=recvs.at[n],
+            device_id=device,
+            device_id_type=MESH,
+        )
+        for n, (source, target, device) in enumerate(routes)
+    ]
+    for copy in copies:
+        copy.start()
+    for copy in copies:
+        copy.wait()
+
+
+def exchange_edges(tiles, other, own_edge, other_edge):
+    hbm = pl.BlockSpec(memory_space=pl.ANY)
+    pieces = 2
+    count = 2 + 2 * pieces
+    return pl.pallas_call(
+        functools.partial(edges_kernel, tiles, pieces),
+        out_shape=tuple(
+            jax.ShapeDtypeStruct(x.shape, x.dtype) for x in (other, own_edge, other_edge)
+        ),
+        in_specs=[hbm] * 3,
+        out_specs=(hbm,) * 3,
+        scratch_shapes=[pltpu.SemaphoreType.DMA((count,)), pltpu.SemaphoreType.DMA((count,))],
+        compiler_params=pltpu.CompilerParams(collective_id=1, has_side_effects=True),
+        name="exchange_edges",
+    )(other, own_edge, other_edge)
 
 
 def patch_kernel(unroll, source_ref, place_ref, real_ref, imag_ref, rows_ref, out_ref, straight, turned, made):
@@ -314,16 +466,11 @@
         sizes, band, plane_index, beam_index, strip_index, cell_row, cell_column, phase_index
     )
     notes = write_notes(key, cell, key_at, cell_at, strips * both)
-    notes = lax.all_to_all(
-        notes.reshape(strips, both), "tile", split_axis=0, concat_axis=0, tiled=True
-    )
-    keys = notes[:, :phase_capacity].reshape(-1)
-    cells = notes[:, phase_capacity:].reshape(-1)
-
-    rows = fetch_rows(keys, kernel_table.reshape(-1, row_width))
-    rows = lax.all_to_all(
-        rows.reshape(strips, phase_capacity, row_width), "tile", split_axis=0, concat_axis=0, tiled=True
-    ).reshape(-1, row_width)
+    got, rows = answer_requests(
+        notes, kernel_table.reshape(-1, row_width), strips, phase_capacity
+    )
+    cells = got.reshape(strips, both)[:, phase_capacity:].reshape(-1)
+    rows = rows.reshape(-1, row_width)
     patches = place_patches(
         source,
         place,
@@ -336,15 +483,9 @@
     ).reshape(-1, row_width)
 
     own, own_edge, other, other_edge = paint(cells, band, patches)
-    bands = lax.axis_size("wband")
-    received = lax.ppermute(other, "wband", [(b, 1 - b) for b in range(bands)])
-    straight = lax.ppermute(own_edge, "tile", [(t, t + 1) for t in range(strips - 1)])
-    crossed = lax.ppermute(
-        other_edge,
-        ("wband", "tile"),
-        [(b * strips + t, (1 - b) * strips + t + 1) for b in range(bands) for t in range(strips - 1)],
-    )
-    edge = jnp.pad(straight + crossed, ((0, 0), (0, ROWS - SUP), (0, 0)))
+    received, straight, crossed = exchange_edges(strips, other, own_edge, other_edge)
+    edge = jnp.where(lax.axis_index("tile") > 0, straight + crossed, 0.0)
+    edge = jnp.pad(edge, ((0, 0), (0, ROWS - SUP), (0, 0)))
     return own + received + edge
 
 

time: 162 us -> 161 us (level)
  Pallas kernels: 60.7 us -> 113 us
  waiting for transfers between devices: 60 us -> 25.1 us
  blocking collectives: 13.9 us -> 0 us
  starting transfers between devices: 12.5 us -> 6.03 us
    pallas_call x1 -> x2, Pallas kernels: 6.59 us -> 59.1 us  [the longest x1 42.2 us: answer_requests(): pl.pallas_call(functools.partial(answer_kernel, tiles, capacity, 16), out...]
    all_to_all x1 -> x0, waiting for transfers between devices: 24.7 us -> none  [local(): lax.all_to_all(rows.reshape(strips, phase_capacity, row_width), 'tile', s...]
    all_to_all x1 -> x0, blocking collectives: 13.9 us -> none  [local(): lax.all_to_all(notes.reshape(strips, both), 'tile', split_axis=0, concat_...]
    ppermute x3 -> x0, waiting for transfers between devices: 10.1 us -> none  [the longest x1 5.23 us: local(): lax.ppermute(other_edge, ('wband', 'tile'), [(b * strips + t, (1 - b) * s...]
    ppermute x3 -> x0, starting transfers between devices: 5.34 us -> none  [the longest x1 3.3 us: local(): lax.ppermute(own_edge, 'tile', [(t, t + 1) for t in range(strips - 1)])]
    all_to_all x1 -> x0, starting transfers between devices: 3.56 us -> none  [local(): lax.all_to_all(rows.reshape(strips, phase_capacity, row_width), 'tile', s...]
    all_to_all x1, starting transfers between devices: 3.56 us -> 6.03 us  [local(): lax.all_to_all(patches.reshape(strips, strip_capacity, row_width), 'tile'...]
    unnamed x30 -> x31, local copies, waits for them, and re-layouts: 9.73 us -> 9.89 us
  transfers between devices with their start and end apart: 5 -> 1, of which waited for: 4 -> 1; matrix products, arithmetic and copies ran while one was open for 0% -> 0% of each run, Pallas kernels for 0% -> 0%
where the time goes in v3:
time: 161 us; the launch traced here: 160 us
  Pallas kernels  113 us (70%)
  waiting for transfers between devices  25.1 us (16%)
  local copies, waits for them, and re-layouts  11.3 us (7%)
  starting transfers between devices  6.03 us (4%)
  other arithmetic  4.21 us (3%)
    pallas_call x1, Pallas kernels, answer_requests(): pl.pallas_call(functools.partial(answer_kernel, tiles, capacity, 16), out...  42.2 us
    pallas_call x1, Pallas kernels, paint(): pl.pallas_call(functools.partial(paint_kernel, 64), out_shape=(main, edge...  35.8 us
    all_to_all x1, waiting for transfers between devices, local(): lax.all_to_all(patches.reshape(strips, strip_capacity, row_width), 'tile'...  25.1 us
    pallas_call x1, Pallas kernels, exchange_edges(): pl.pallas_call(functools.partial(edges_kernel, tiles, pieces), out_shape=...  16.9 us
    pallas_call x1, Pallas kernels, write_notes(): pl.pallas_call(functools.partial(notes_kernel, 16), out_shape=jax.ShapeDt...  10.2 us
    unnamed x31, local copies, waits for them, and re-layouts  9.89 us
    pallas_call x1, Pallas kernels, place_patches(): pl.pallas_call(functools.partial(patch_kernel, 16), out_shape=jax.ShapeDt...  7.8 us
    all_to_all x1, starting transfers between devices, local(): lax.all_to_all(patches.reshape(strips, strip_capacity, row_width), 'tile'...  6.03 us
  transfers between devices with their start and end apart: 1, of which 1 were waited for; matrix products, arithmetic and copies ran while one was open for 0% of the time, Pallas kernels for 0%

profile of v3, /device:TPU:0, one launch (start us, length us, event | category | flops | bytes accessed | tf_op | source)
XLA Modules:
  0.0 160.0 jit_solution(9088188731132903430)
XLA Ops:
  0.0 0.8 fusion
  0.8 0.0 copy-start.2
  0.8 0.7 copy-done.2
  1.5 0.0 copy-start.3
  1.5 0.7 copy-done.3
  2.2 0.0 copy-start.4
  2.2 0.7 copy-done.4
  2.9 0.0 copy-start.5
  2.9 0.7 copy-done.5
  3.6 0.0 copy-start.6
  3.6 0.7 copy-done.6
  4.3 0.0 copy-start.7
  4.3 0.7 copy-done.7
  5.0 0.3 addresses.1
  5.3 0.0 copy-start.8
  5.3 0.6 copy-done.8
  5.9 0.0 copy-start.9
  5.9 0.6 copy-done.9
  6.5 0.0 copy-start.10
  6.5 0.6 copy-done.10
  7.1 0.0 copy-start.11
  7.1 0.6 broadcast_in_dim.7.blank_ref
  7.7 0.0 copy-done.11
  7.7 10.2 %write_notes.1 = s32[8192]{0:T(1024)} custom-call(s32[2048]{0:T(1024)} %bitcast.41, s32[2048]{0:T(1024)} %bitcast.42, s32[2048]{0:T(1024)} %bitcast.43, s32[2048]{0:T(1024)} %bitcast.44, s32[8192]{0:T(1024)} %broadcast_in_dim.7.blank_ref), custom_call_target="tpu_custom_call" | custom-call | tf_op jit(solution)/shard_map/write_notes/pallas_call | solution.py:99
  17.9 0.0 copy-start
  17.9 1.6 copy-done
  19.5 0.0 copy-start.1
  19.5 0.8 copy-done.1
  20.3 42.2 %answer_requests.1 = (s32[8,8,128]{2,1,0:T(8,128)S(1)}, bf16[8,512,128]{2,1,0:T(8,128)(2,1)S(1)}) custom-call(s32[8,8,128]{2,1,0:T(8,128)S(1)} %bitcast.29, bf16[8192,128]{1,0:T(8,128)(2,1)S(1)} %bitcast.27), custom_call_target="tpu_custom_call" | custom-call | tf_op jit(solution)/shard_map/answer_requests/pallas_call | solution.py:214
  62.5 7.8 %place_patches.1 = bf16[4096,128]{1,0:T(8,128)(2,1)} custom-call(s32[2048]{0:T(1024)S(1)} %bitcast.33, s32[2048]{0:T(1024)S(1)} %bitcast.34, f32[2048]{0:T(1024)S(1)} %bitcast.31, f32[2048]{0:T(1024)S(1)} %bitcast.30, bf16[4096,128]{1,0:T(8,128)(2,1)S(1)} %bitcast.28), custom_call_target="tpu_custom_call" | custom-call | tf_op jit(solution)/shard_map/place_patches/pallas_call | solution.py:317
  70.3 6.0 %all-to-all-start = ((bf16[8,512,128]{2,1,0:T(8,128)(2,1)}), bf16[8,512,128]{2,1,0:T(8,128)(2,1)S(1)}, u32[]{:S(2)}, u32[]{:S(2)}) async-start(bf16[8,512,128]{2,1,0:T(8,128)(2,1)} %bitcast.18), calls=%async_computation | async-start | bytes 2097152 | tf_op jit(solution)/shard_map/all_to_all | solution.py:481
  76.3 0.6 copy.10
  76.9 25.1 %all-to-all-done = bf16[8,512,128]{2,1,0:T(8,128)(2,1)S(1)} async-done(((bf16[8,512,128]{2,1,0:T(8,128)(2,1)}), bf16[8,512,128]{2,1,0:T(8,128)(2,1)S(1)}, u32[]{:S(2)}, u32[]{:S(2)}) %all-to-all-start) | async-done | bytes 1048608 | tf_op jit(solution)/shard_map/all_to_all | solution.py:481
  102.1 0.0 copy-start.12
  102.1 1.0 copy-done.12
  103.0 35.8 %paint.1 = (f32[2,64,4096]{2,1,0:T(8,128)}, f32[2,8,4096]{2,1,0:T(8,128)}, f32[2,64,4096]{2,1,0:T(8,128)}, f32[2,8,4096]{2,1,0:T(8,128)}) custom-call(s32[4096]{0:T(1024)} %bitcast.47, s32[1]{0:T(128)} %bitcast.band_ref, bf16[4096,128]{1,0:T(8,128)(2,1)} %bitcast.45), custom_call_target="tpu_custom_call" | custom-call | tf_op jit(solution)/shard_map/paint/pallas_call | solution.py:432
  138.8 0.0 copy-start.13
  138.9 16.9 %exchange_edges.1 = (f32[2,64,4096]{2,1,0:T(8,128)}, f32[2,8,4096]{2,1,0:T(8,128)}, f32[2,8,4096]{2,1,0:T(8,128)}) custom-call(f32[2,64,4096]{2,1,0:T(8,128)} %get-tuple-element.29.other_ref, f32[2,8,4096]{2,1,0:T(8,128)} %get-tuple-element.30.own_edge_ref, f32[2,8,4096]{2,1,0:T(8,128)} %get-tuple-element.31.other_edge_ref), custom_call_target="tpu_custom_call" | custom-call | tf_op jit(solution)/shard_map/exchange_edges/pallas_call | solution.py:279
  155.8 1.1 add_select_fusion
  156.8 0.0 copy-done.13
  156.8 3.1 %pad_add_fusion = f32[2,64,4096]{2,1,0:T(8,128)} fusion(f32[2,8,4096]{2,1,0:T(8,128)S(1)} %add_select_fusion, f32[2,64,4096]{2,1,0:T(8,128)S(1)} %copy-done.13, f32[2,64,4096]{2,1,0:T(8,128)} %get-tuple-element.32), kind=kLoop, calls=%fused_computation | loop fusion | flops 1048576 | bytes 6553600 | tf_op jit(solution)/shard_map/add | solution.py:489
  (2 shorter events, 0.0 us)
Async XLA Ops:
  0.8 0.7 copy-start.2
  1.5 0.7 copy-start.3
  2.2 0.7 copy-start.4
  2.9 0.7 copy-start.5
  3.6 0.7 copy-start.6
  4.3 0.7 copy-start.7
  5.3 0.6 copy-start.8
  5.9 0.6 copy-start.9
  6.5 0.6 copy-start.10
  7.1 0.6 copy-start.11
  17.9 1.6 copy-start
  19.5 0.8 copy-start.1
  70.3 31.8 %all-to-all-start = ((bf16[8,512,128]{2,1,0:T(8,128)(2,1)}), bf16[8,512,128]{2,1,0:T(8,128)(2,1)S(1)}, u32[]{:S(2)}, u32[]{:S(2)}) async-start(bf16[8,512,128]{2,1,0:T(8,128)(2,1)} %bitcast.18), calls=%async_computation | async-start | bytes 2097152 | tf_op jit(solution)/shard_map/all_to_all | solution.py:481
  102.1 1.0 copy-start.12
  138.8 18.0 %copy-start.13 = (f32[2,64,4096]{2,1,0:T(8,128)S(1)}, f32[2,64,4096]{2,1,0:T(8,128)}, u32[]{:S(2)}) copy-start(f32[2,64,4096]{2,1,0:T(8,128)} %get-tuple-element.28) | copy-start | bytes 6291460

commit v4 on v3

--- a/solution.py
+++ b/solution.py
@@ -44,66 +44,90 @@
     return jnp.sum(ranks.reshape(buckets, rows, LANES), axis=0).astype(jnp.int32)
 
 
+def spread_to_slots(position, total, *pieces):
+    high_count = total // LANES
+    high, low = position // LANES, position % LANES
+    high_slot = lax.broadcasted_iota(jnp.int32, (high_count, LANES), 0)
+    low_slot = lax.broadcasted_iota(jnp.int32, (LANES, LANES), 0)
+    sums = jnp.zeros((len(pieces) * high_count, LANES), jnp.float32)
+    for a in range(position.shape[0]):
+        at_high = high[a : a + 1] == high_slot
+        values = [jnp.where(at_high, piece[a : a + 1], 0.0) for piece in pieces]
+        left = jnp.concatenate(values, axis=0).astype(jnp.bfloat16)
+        right = jnp.where(low[a : a + 1] == low_slot, 1.0, 0.0).astype(jnp.bfloat16)
+        sums = sums + lax.dot_general(
+            left, right, (((1,), (1,)), ((), ())), preferred_element_type=jnp.float32
+        )
+    return [sums[i * high_count : (i + 1) * high_count] for i in range(len(pieces))]
+
+
+def bytes_of(values):
+    return [((values >> shift) & 255).astype(jnp.float32) for shift in (16, 8, 0)]
+
+
+def from_bytes(top, middle, bottom):
+    return (top * 65536.0 + middle * 256.0 + bottom).astype(jnp.int32)
+
+
+def thirds_of(values):
+    top = values.astype(jnp.bfloat16).astype(jnp.float32)
+    rest = values - top
+    middle = rest.astype(jnp.bfloat16).astype(jnp.float32)
+    return [top, middle, rest - middle]
+
+
 def address_kernel(
-    sizes, band_ref, plane_ref, beam_ref, strip_ref, row_ref, column_ref, phase_ref,
-    key_ref, cell_ref, source_ref, place_ref, key_at_ref, cell_at_ref,
+    sizes, band_ref, plane_ref, beam_ref, strip_ref, row_ref, column_ref, phase_ref, real_ref, imag_ref,
+    notes_ref, source_ref, slot_real_ref, slot_imag_ref,
 ):
     strips, planes_band, beam_count, phase_local, phase_capacity, strip_capacity = sizes
     both = phase_capacity + strip_capacity
     phase, strip, column = phase_ref[...], strip_ref[...], column_ref[...]
     owner = phase // phase_local
     key = ((plane_ref[...] - band_ref[0] * planes_band) * beam_count + beam_ref[...]) * phase_local
-    key_ref[...] = key + (phase - owner * phase_local)
+    key = key + (phase - owner * phase_local)
     tile_row = ((column >> SHIFT) + 1) * HEIGHT + row_ref[...]
-    cell_ref[...] = tile_row * STRIDE + (column & (STRIDE - 1))
+    cell = tile_row * STRIDE + (column & (STRIDE - 1))
     owner_rank = rank_in_bucket(owner, strips)
     strip_rank = rank_in_bucket(strip, strips)
-    source_ref[...] = owner * phase_capacity + owner_rank
-    place_ref[...] = strip * strip_capacity + strip_rank
-    key_at_ref[...] = owner * both + owner_rank
-    cell_at_ref[...] = strip * both + phase_capacity + strip_rank
+    total = strips * both
+    keys = spread_to_slots(owner * both + owner_rank, total, *bytes_of(key))
+    cells = spread_to_slots(strip * both + phase_capacity + strip_rank, total, *bytes_of(cell))
+    notes_ref[...] = from_bytes(*(k + c for k, c in zip(keys, cells)))
+    slots = spread_to_slots(
+        strip * strip_capacity + strip_rank,
+        strips * strip_capacity,
+        *bytes_of(owner * phase_capacity + owner_rank),
+        *thirds_of(real_ref[...]),
+        *thirds_of(imag_ref[...]),
+    )
+    source_ref[...] = from_bytes(*slots[:3])
+    slot_real_ref[...] = slots[3] + slots[4] + slots[5]
+    slot_imag_ref[...] = slots[6] + slots[7] + slots[8]
 
 
 def addresses(sizes, band, *columns):
+    strips, _, _, _, phase_capacity, strip_capacity = sizes
     blocks = columns[0].shape[0]
-    shape = jax.ShapeDtypeStruct((blocks // LANES, LANES), jnp.int32)
+    slots = strips * strip_capacity
     vmem = pl.BlockSpec(memory_space=pltpu.VMEM)
-    results = pl.pallas_call(
+
+    def shape(count, kind):
+        return jax.ShapeDtypeStruct((count // LANES, LANES), kind)
+
+    return pl.pallas_call(
         functools.partial(address_kernel, sizes),
-        out_shape=(shape,) * 6,
+        out_shape=(
+            shape(strips * phase_capacity + slots, jnp.int32),
+            shape(slots, jnp.int32),
+            shape(slots, jnp.float32),
+            shape(slots, jnp.float32),
+        ),
         in_specs=[pl.BlockSpec(memory_space=pltpu.SMEM)] + [vmem] * len(columns),
-        out_specs=(vmem,) * 6,
+        out_specs=(vmem,) * 4,
         compiler_params=pltpu.CompilerParams(vmem_limit_bytes=40 * 2**20),
         name="addresses",
-    )(band, *(column.reshape(shape.shape) for column in columns))
-    return [result.reshape(blocks) for result in results]
-
-
-def notes_kernel(unroll, key_ref, cell_ref, key_at_ref, cell_at_ref, blank_ref, out_ref, sem):
-    copy = pltpu.make_async_copy(blank_ref, out_ref, sem)
-    copy.start()
-    copy.wait()
-
-    def body(i, carry):
-        for u in range(unroll):
-            n = i * unroll + u
-            out_ref[key_at_ref[n]] = key_ref[n]
-            out_ref[cell_at_ref[n]] = cell_ref[n]
-        return carry
-
-    lax.fori_loop(0, key_ref.shape[0] // unroll, body, 0)
-
-
-def write_notes(key, cell, key_at, cell_at, total):
-    smem = pl.BlockSpec(memory_space=pltpu.SMEM)
-    return pl.pallas_call(
-        functools.partial(notes_kernel, 16),
-        out_shape=jax.ShapeDtypeStruct((total,), jnp.int32),
-        in_specs=[smem] * 4 + [pl.BlockSpec(memory_space=pl.ANY)],
-        out_specs=smem,
-        scratch_shapes=[pltpu.SemaphoreType.DMA],
-        name="write_notes",
-    )(key, cell, key_at, cell_at, jnp.zeros((total,), jnp.int32))
+    )(band, *(column.reshape(blocks // LANES, LANES) for column in columns))
 
 
 def peer(me, step, count):
@@ -128,6 +152,11 @@
 
     lax.fori_loop(1, tiles, body, 0)
     return barrier
+
+
+def far_first(k, tiles):
+    up, down = tiles // 2 + k // 2, tiles // 2 - (k + 1) // 2
+    return jnp.where(k % 2 == 0, up, down)
 
 
 def answer_kernel(
@@ -187,12 +216,13 @@
         lax.fori_loop(0, capacity // unroll, body, 0)
         outgoing[target] = picked[...].astype(jnp.bfloat16)
 
-    def send_rows(step, carry):
+    def send_rows(k, carry):
+        step = far_first(k, tiles)
         look_up(peer(me, step, tiles))
         row_copy(step, me).start()
         return carry
 
-    lax.fori_loop(1, tiles, send_rows, 0)
+    lax.fori_loop(0, tiles - 1, send_rows, 0)
     look_up(me)
     keep = pltpu.make_async_copy(outgoing.at[me], rows_ref.at[me], own_sem)
     keep.start()
@@ -289,44 +319,94 @@
     )(other, own_edge, other_edge)
 
 
-def patch_kernel(unroll, source_ref, place_ref, real_ref, imag_ref, rows_ref, out_ref, straight, turned, made):
-    wide = rows_ref[...].astype(jnp.float32)
-    straight[...] = wide
-    lane = lax.broadcasted_iota(jnp.int32, wide.shape, 1)
-    swapped = pltpu.roll(wide, HALF, 1)
-    turned[...] = jnp.where(lane < HALF, -swapped, swapped)
-    made[...] = jnp.zeros_like(made)
-
-    def body(i, carry):
-        for u in range(unroll):
-            n = i * unroll + u
-            row = pl.ds(source_ref[n], 1)
-            made[pl.ds(place_ref[n], 1), :] = (
-                real_ref[n] * straight[row, :] + imag_ref[n] * turned[row, :]
-            )
-        return carry
-
-    lax.fori_loop(0, source_ref.shape[0] // unroll, body, 0)
-    out_ref[...] = made[...].astype(jnp.bfloat16)
-
-
-def place_patches(source, place, visibility, rows, slots):
-    width = rows.shape[1]
-    smem = pl.BlockSpec(memory_space=pltpu.SMEM)
+def patch_kernel(
+    tiles, unroll, source_ref, real_ref, imag_ref, rows_ref, patches_ref,
+    wide, real_scale, imag_scale, picked, outgoing, sends, recvs, own_sem,
+):
+    me = lax.axis_index("tile")
+    barrier = greet_tiles(me, tiles)
+    wide[...] = rows_ref[...].astype(jnp.float32)
+
+    def scale(g, carry):
+        at = pl.ds(pl.multiple_of(g * LANES, LANES), LANES)
+        for values, scales in ((real_ref, real_scale), (imag_ref, imag_scale)):
+            scales[at, :] = jnp.broadcast_to(values[pl.ds(g, 1), :], (LANES, LANES)).T
+        return carry
+
+    lax.fori_loop(0, real_ref.shape[0], scale, 0)
+    pl.semaphore_wait(barrier, tiles - 1)
+    capacity = picked.shape[0]
+    lane = lax.broadcasted_iota(jnp.int32, picked.shape, 1)
+
+    def copy(step, sender):
+        target = peer(me, step, tiles)
+        return pltpu.make_async_remote_copy(
+            src_ref=outgoing.at[target],
+            dst_ref=patches_ref.at[sender],
+            send_sem=sends.at[step],
+            recv_sem=recvs.at[step],
+            device_id={"tile": target},
+            device_id_type=MESH,
+        )
+
+    def make(target):
+        def body(i, carry):
+            for u in range(unroll):
+                j = i * unroll + u
+                picked[pl.ds(j, 1), :] = wide[pl.ds(source_ref[target * capacity + j], 1), :]
+            return carry
+
+        lax.fori_loop(0, capacity // unroll, body, 0)
+        at = pl.ds(pl.multiple_of(target * capacity, capacity), capacity)
+        straight = picked[...]
+        swapped = pltpu.roll(straight, HALF, 1)
+        turned = jnp.where(lane < HALF, -swapped, swapped)
+        made = real_scale[at, :] * straight + imag_scale[at, :] * turned
+        outgoing[target] = made.astype(jnp.bfloat16)
+
+    def send(k, carry):
+        step = far_first(k, tiles)
+        make(peer(me, step, tiles))
+        copy(step, me).start()
+        return carry
+
+    lax.fori_loop(0, tiles - 1, send, 0)
+    make(me)
+    keep = pltpu.make_async_copy(outgoing.at[me], patches_ref.at[me], own_sem)
+    keep.start()
+
+    def finish(step, carry):
+        copy(step, peer(me, -step, tiles)).wait()
+        return carry
+
+    lax.fori_loop(1, tiles, finish, 0)
+    keep.wait()
+
+
+def send_patches(source, real, imag, rows, tiles):
+    slots, width = real.size, rows.shape[1]
+    capacity = slots // tiles
     vmem = pl.BlockSpec(memory_space=pltpu.VMEM)
     return pl.pallas_call(
-        functools.partial(patch_kernel, 16),
-        out_shape=jax.ShapeDtypeStruct((slots, width), jnp.bfloat16),
-        in_specs=[smem, smem, smem, smem, vmem],
-        out_specs=vmem,
+        functools.partial(patch_kernel, tiles, 16),
+        out_shape=jax.ShapeDtypeStruct((tiles, capacity, width), jnp.bfloat16),
+        in_specs=[pl.BlockSpec(memory_space=pltpu.SMEM), vmem, vmem, vmem],
+        out_specs=pl.BlockSpec(memory_space=pl.ANY),
         scratch_shapes=[
             pltpu.VMEM(rows.shape, jnp.float32),
-            pltpu.VMEM(rows.shape, jnp.float32),
             pltpu.VMEM((slots, width), jnp.float32),
+            pltpu.VMEM((slots, width), jnp.float32),
+            pltpu.VMEM((capacity, width), jnp.float32),
+            pltpu.VMEM((tiles, capacity, width), jnp.bfloat16),
+            pltpu.SemaphoreType.DMA((tiles,)),
+            pltpu.SemaphoreType.DMA((tiles,)),
+            pltpu.SemaphoreType.DMA,
         ],
-        compiler_params=pltpu.CompilerParams(vmem_limit_bytes=40 * 2**20),
-        name="place_patches",
-    )(source, place, visibility[:, 0], visibility[:, 1], rows)
+        compiler_params=pltpu.CompilerParams(
+            collective_id=2, has_side_effects=True, vmem_limit_bytes=40 * 2**20
+        ),
+        name="send_patches",
+    )(source.reshape(-1), real, imag, rows)
 
 
 def paint_kernel(
@@ -392,6 +472,7 @@
         def column(b, carry):
             first = (start_block + b) * per_block
             at = pl.ds(pl.multiple_of(b * LANES, LANES), LANES)
+            merged = []
             for p in range(HEIGHT // SUP):
                 tiles = []
                 for t in range(per_block + 1):
@@ -408,13 +489,13 @@
                 imag = jnp.where(lower, pltpu.roll(t0, HALF, 1), t2) + jnp.where(
                     middle, pltpu.roll(t1, LANES - STRIDE, 1), pltpu.roll(edges, STRIDE, 1)
                 )
-                if p < ROWS // SUP:
-                    rows = slice(p * SUP, (p + 1) * SUP)
-                    main_ref[0, rows, at] = real
-                    main_ref[1, rows, at] = imag
-                else:
-                    edge_ref[0, :, at] = real
-                    edge_ref[1, :, at] = imag
+                merged.append((real, imag))
+            for p in range(0, ROWS // SUP, 2):
+                rows = slice(p * SUP, (p + 2) * SUP)
+                for k in range(2):
+                    pair = jnp.concatenate([merged[p][k], merged[p + 1][k]], axis=0)
+                    main_ref[k, rows, at] = pair.astype(main_ref.dtype)
+            edge_ref[:, at] = jnp.concatenate(merged[-1], axis=0).astype(edge_ref.dtype)
             return carry
 
         lax.fori_loop(0, blocks, column, 0)
@@ -426,12 +507,13 @@
 
 def paint(cells, band, patches):
     main = jax.ShapeDtypeStruct((2, ROWS, NV // 2), jnp.float32)
-    edge = jax.ShapeDtypeStruct((2, SUP, NV // 2), jnp.float32)
+    other = jax.ShapeDtypeStruct(main.shape, jnp.bfloat16)
+    edge = jax.ShapeDtypeStruct((2 * SUP, NV // 2), jnp.bfloat16)
     smem = pl.BlockSpec(memory_space=pltpu.SMEM)
     vmem = pl.BlockSpec(memory_space=pltpu.VMEM)
     return pl.pallas_call(
         functools.partial(paint_kernel, 64),
-        out_shape=(main, edge, main, edge),
+        out_shape=(main, edge, other, edge),
         in_specs=[smem, smem, vmem],
         out_specs=(vmem, vmem, vmem, vmem),
         scratch_shapes=[pltpu.VMEM((patches.shape[0] * SUP, LANES), jnp.float32)]
@@ -462,31 +544,23 @@
 
     band = band_index.reshape(1).astype(jnp.int32)
     sizes = (strips, planes_band, beam_count, phase_local, phase_capacity, strip_capacity)
-    key, cell, source, place, key_at, cell_at = addresses(
-        sizes, band, plane_index, beam_index, strip_index, cell_row, cell_column, phase_index
-    )
-    notes = write_notes(key, cell, key_at, cell_at, strips * both)
+    notes, source, slot_real, slot_imag = addresses(
+        sizes, band, plane_index, beam_index, strip_index, cell_row, cell_column, phase_index,
+        visibility[:, 0], visibility[:, 1],
+    )
     got, rows = answer_requests(
         notes, kernel_table.reshape(-1, row_width), strips, phase_capacity
     )
     cells = got.reshape(strips, both)[:, phase_capacity:].reshape(-1)
-    rows = rows.reshape(-1, row_width)
-    patches = place_patches(
-        source,
-        place,
-        visibility,
-        rows,
-        strips * strip_capacity,
-    )
-    patches = lax.all_to_all(
-        patches.reshape(strips, strip_capacity, row_width), "tile", split_axis=0, concat_axis=0, tiled=True
-    ).reshape(-1, row_width)
+    patches = send_patches(source, slot_real, slot_imag, rows.reshape(-1, row_width), strips)
+    patches = patches.reshape(-1, row_width)
 
     own, own_edge, other, other_edge = paint(cells, band, patches)
     received, straight, crossed = exchange_edges(strips, other, own_edge, other_edge)
-    edge = jnp.where(lax.axis_index("tile") > 0, straight + crossed, 0.0)
+    edge = straight.astype(jnp.float32) + crossed.astype(jnp.float32)
+    edge = jnp.where(lax.axis_index("tile") > 0, edge, 0.0).reshape(2, SUP, -1)
     edge = jnp.pad(edge, ((0, 0), (0, ROWS - SUP), (0, 0)))
-    return own + received + edge
+    return own + received.astype(jnp.float32) + edge
 
 
 def solution(mesh):

time: 161 us -> 130 us (0.81)
  waiting for transfers between devices: 25.1 us -> 0 us
  starting transfers between devices: 6.03 us -> 0 us
  Pallas kernels: 113 us -> 117 us
  local copies, waits for them, and re-layouts: 11.3 us -> 8.19 us
    all_to_all x1 -> x0, waiting for transfers between devices: 25.1 us -> none  [local(): lax.all_to_all(patches.reshape(strips, strip_capacity, row_width), 'tile'...]
    pallas_call x2 -> x1, Pallas kernels: 18 us -> 24.8 us  [send_patches(): pl.pallas_call(functools.partial(patch_kernel, tiles, 16), out_shape=jax....]
    all_to_all x1 -> x0, starting transfers between devices: 6.03 us -> none  [local(): lax.all_to_all(patches.reshape(strips, strip_capacity, row_width), 'tile'...]
    pallas_call x1, Pallas kernels: 16.9 us -> 11.8 us  [exchange_edges(): pl.pallas_call(functools.partial(edges_kernel, tiles, pieces), out_shape=...]
    unnamed x31 -> x19, local copies, waits for them, and re-layouts: 9.89 us -> 7.38 us
  transfers between devices with their start and end apart: 1 -> 0, of which waited for: 1 -> 0; matrix products, arithmetic and copies ran while one was open for 0% -> 0% of each run, Pallas kernels for 0% -> 0%
where the time goes in v4:
time: 130 us
  Pallas kernels  117 us (90%)
  local copies, waits for them, and re-layouts  8.19 us (6%)
  other arithmetic  4.43 us (3%)
    pallas_call x1, Pallas kernels, answer_requests(): pl.pallas_call(functools.partial(answer_kernel, tiles, capacity, 16), out...  43.4 us
    pallas_call x1, Pallas kernels, paint(): pl.pallas_call(functools.partial(paint_kernel, 64), out_shape=(main, edge...  35.4 us
    pallas_call x1, Pallas kernels, send_patches(): pl.pallas_call(functools.partial(patch_kernel, tiles, 16), out_shape=jax....  24.8 us
    pallas_call x1, Pallas kernels, exchange_edges(): pl.pallas_call(functools.partial(edges_kernel, tiles, pieces), out_shape=...  11.8 us
    unnamed x19, local copies, waits for them, and re-layouts  7.38 us
    add x1, other arithmetic, local(): return own + received.astype(jnp.float32) + edge  3.42 us

profile of v4, /device:TPU:0, one launch (start us, length us, event | category | flops | bytes accessed | tf_op | source)
XLA Modules:
  0.0 129.6 jit_solution(11247598019761010886)
XLA Ops:
  0.0 0.8 fusion
  0.8 0.0 copy-start.2
  0.8 0.7 copy-done.2
  1.5 0.0 copy-start.3
  1.5 0.7 copy-done.3
  2.2 0.0 copy-start.4
  2.2 0.7 copy-done.4
  2.9 0.0 copy-start.5
  2.9 0.7 copy-done.5
  3.6 0.0 copy-start.6
  3.6 0.7 copy-done.6
  4.3 0.0 copy-start.7
  4.3 0.7 copy-done.7
  5.0 1.5 %addresses.1 = (s32[64,128]{1,0:T(8,128)S(1)}, s32[32,128]{1,0:T(8,128)S(1)}, f32[32,128]{1,0:T(8,128)S(1)}, f32[32,128]{1,0:T(8,128)S(1)}) custom-call(s32[1]{0:T(128)} %bitcast.band_ref, s32[16,128]{1,0:T(8,128)S(1)} %bitcast.31, s32[16,128]{1,0:T(8,128)S(1)} %bitcast.32, s32[16,128]{1,0:T(8,128)S(1)} %bitcast.33, s32[16,128]{1,0:T(8,128)S(1)} %bitcast.34, ...), custom_call_target="tpu_custom_call" | custom-call | tf_op jit(solution)/shard_map/addresses/pallas_call | solution.py:118
  6.5 0.0 copy-start.1
  6.5 1.6 %copy-done.1 = bf16[32,32,8,128]{3,2,1,0:T(8,128)(2,1)S(1)} copy-done((bf16[32,32,8,128]{3,2,1,0:T(8,128)(2,1)S(1)}, bf16[32,32,8,128]{3,2,1,0:T(8,128)(2,1)}, u32[]{:S(2)}) %copy-start.1) | copy-done | bytes 2097176
  8.1 43.4 %answer_requests.1 = (s32[8,8,128]{2,1,0:T(8,128)S(1)}, bf16[8,512,128]{2,1,0:T(8,128)(2,1)S(1)}) custom-call(s32[8,8,128]{2,1,0:T(8,128)S(1)} %bitcast.26, bf16[8192,128]{1,0:T(8,128)(2,1)S(1)} %bitcast.24), custom_call_target="tpu_custom_call" | custom-call | tf_op jit(solution)/shard_map/answer_requests/pallas_call | solution.py:244
  51.5 0.6 copy.10
  52.1 24.8 %send_patches.1 = bf16[8,512,128]{2,1,0:T(8,128)(2,1)S(1)} custom-call(s32[4096]{0:T(1024)S(1)} %bitcast.30, f32[32,128]{1,0:T(8,128)S(1)} %get-tuple-element.21.real_ref, f32[32,128]{1,0:T(8,128)S(1)} %get-tuple-element.22.imag_ref, bf16[4096,128]{1,0:T(8,128)(2,1)S(1)} %bitcast.25), custom_call_target="tpu_custom_call" | custom-call | tf_op jit(solution)/shard_map/send_patches/pallas_call | solution.py:390
  76.9 0.0 copy-start
  76.9 1.0 copy-done
  77.9 35.4 %paint.1 = (f32[2,64,4096]{2,1,0:T(8,128)}, bf16[16,4096]{1,0:T(8,128)(2,1)}, bf16[2,64,4096]{2,1,0:T(8,128)(2,1)}, bf16[16,4096]{1,0:T(8,128)(2,1)}) custom-call(s32[4096]{0:T(1024)} %bitcast.38, s32[1]{0:T(128)} %bitcast.band_ref, bf16[4096,128]{1,0:T(8,128)(2,1)} %bitcast.23), custom_call_target="tpu_custom_call" | custom-call | tf_op jit(solution)/shard_map/paint/pallas_call | solution.py:514
  113.3 11.8 %exchange_edges.1 = (bf16[2,64,4096]{2,1,0:T(8,128)(2,1)}, bf16[16,4096]{1,0:T(8,128)(2,1)}, bf16[16,4096]{1,0:T(8,128)(2,1)}) custom-call(bf16[2,64,4096]{2,1,0:T(8,128)(2,1)} %get-tuple-element.25.other_ref, bf16[16,4096]{1,0:T(8,128)(2,1)} %get-tuple-element.26.own_edge_ref, bf16[16,4096]{1,0:T(8,128)(2,1)} %get-tuple-element.27.other_edge_ref), custom_call_target="tpu_custom_call" | custom-call | tf_op jit(solution)/shard_map/exchange_edges/pallas_call | solution.py:309
  125.1 1.0 select_bitcast_fusion
  126.1 3.4 %pad_add_fusion = f32[2,64,4096]{2,1,0:T(8,128)} fusion(f32[2,8,4096]{2,1,0:T(8,128)S(1)} %select_bitcast_fusion, f32[2,64,4096]{2,1,0:T(8,128)} %get-tuple-element.24, bf16[2,64,4096]{2,1,0:T(8,128)(2,1)} %get-tuple-element.28), kind=kLoop, calls=%fused_computation | loop fusion | flops 1572864 | bytes 5505024 | tf_op jit(solution)/shard_map/add | solution.py:563
  (2 shorter events, 0.0 us)
Async XLA Ops:
  0.8 0.7 copy-start.2
  1.5 0.7 copy-start.3
  2.2 0.7 copy-start.4
  2.9 0.7 copy-start.5
  3.6 0.7 copy-start.6
  4.3 0.7 copy-start.7
  6.5 1.6 %copy-start.1 = (bf16[32,32,8,128]{3,2,1,0:T(8,128)(2,1)S(1)}, bf16[32,32,8,128]{3,2,1,0:T(8,128)(2,1)}, u32[]{:S(2)}) copy-start(bf16[32,32,8,128]{3,2,1,0:T(8,128)(2,1)} %param.15) | copy-start | bytes 6291460
  76.9 1.0 copy-start

commit v5 on v4

--- a/solution.py
+++ b/solution.py
@@ -1,4 +1,5 @@
 import functools
+import math
 
 import jax
 import jax.numpy as jnp
@@ -159,36 +160,35 @@
     return jnp.where(k % 2 == 0, up, down)
 
 
-def answer_kernel(
-    tiles, capacity, unroll, notes_ref, table_ref, got_ref, rows_ref,
-    wide, picked, outgoing, listed, note_send, note_recv, row_send, row_recv, own_sem,
+def trade_kernel(
+    tiles, phase_capacity, strip_capacity, unroll,
+    source_ref, notes_ref, table_ref, real_ref, imag_ref, got_ref, patches_ref,
+    table, wide, picked, outgoing, incoming, straight, real_scale, imag_scale, chosen, leaving, listed,
+    note_send, note_recv, row_send, row_recv, patch_send, patch_recv, table_sem, own_sem,
 ):
     me = lax.axis_index("tile")
     barrier = greet_tiles(me, tiles)
-    wide[...] = table_ref[...].astype(jnp.float32)
+    fetch_table = pltpu.make_async_copy(table_ref, table, table_sem)
+    fetch_table.start()
     pl.semaphore_wait(barrier, tiles - 1)
 
-    def note_copy(step, sender):
-        target = peer(me, step, tiles)
-        return pltpu.make_async_remote_copy(
-            src_ref=notes_ref.at[target],
-            dst_ref=got_ref.at[sender],
-            send_sem=note_send.at[step],
-            recv_sem=note_recv.at[step],
-            device_id={"tile": target},
-            device_id_type=MESH,
-        )
-
-    def row_copy(step, sender):
-        target = peer(me, step, tiles)
-        return pltpu.make_async_remote_copy(
-            src_ref=outgoing.at[target],
-            dst_ref=rows_ref.at[sender],
-            send_sem=row_send.at[step],
-            recv_sem=row_recv.at[step],
-            device_id={"tile": target},
-            device_id_type=MESH,
-        )
+    def copier(source, target_ref, sends, recvs):
+        def copy(step, sender):
+            target = peer(me, step, tiles)
+            return pltpu.make_async_remote_copy(
+                src_ref=source.at[target],
+                dst_ref=target_ref.at[sender],
+                send_sem=sends.at[step],
+                recv_sem=recvs.at[step],
+                device_id={"tile": target},
+                device_id_type=MESH,
+            )
+
+        return copy
+
+    note_copy = copier(notes_ref, got_ref, note_send, note_recv)
+    row_copy = copier(outgoing, incoming, row_send, row_recv)
+    patch_copy = copier(leaving, patches_ref, patch_send, patch_recv)
 
     def start_notes(step, carry):
         note_copy(step, me).start()
@@ -200,71 +200,133 @@
 
     lax.fori_loop(1, tiles, start_notes, 0)
     got_ref[me] = notes_ref[me]
+    fetch_table.wait()
+    wide[...] = table[...].astype(jnp.float32)
     lax.fori_loop(1, tiles, wait_notes, 0)
     listing = pltpu.make_async_copy(got_ref, listed, own_sem)
     listing.start()
     listing.wait()
+    groups = LANES // unroll
+    group_shift = groups.bit_length() - 1
 
     def look_up(target):
+        def body(i, carry):
+            line, lane = i >> group_shift, (i & (groups - 1)) * unroll
+            for u in range(unroll):
+                key = listed[target, line, lane + u]
+                picked[pl.ds(i * unroll + u, 1), :] = wide[pl.ds(key, 1), :]
+            return carry
+
+        lax.fori_loop(0, phase_capacity // unroll, body, 0)
+        return picked[...]
+
+    def send_rows(k, carry):
+        step = far_first(k, tiles)
+        target = peer(me, step, tiles)
+        outgoing[target] = look_up(target).astype(jnp.bfloat16)
+        row_copy(step, me).start()
+        return carry
+
+    lax.fori_loop(0, tiles - 1, send_rows, 0)
+
+    def rows_of(tile):
+        return pl.ds(pl.multiple_of(tile * phase_capacity, phase_capacity), phase_capacity)
+
+    straight[rows_of(me), :] = look_up(me)
+
+    def scale(g, carry):
+        at = pl.ds(pl.multiple_of(g * LANES, LANES), LANES)
+        for values, scales in ((real_ref, real_scale), (imag_ref, imag_scale)):
+            scales[at, :] = jnp.broadcast_to(values[pl.ds(g, 1), :], (LANES, LANES)).T
+        return carry
+
+    lax.fori_loop(0, real_ref.shape[0], scale, 0)
+
+    def take_rows(k, carry):
+        step = tiles - 1 - k
+        sender = peer(me, -step, tiles)
+        row_copy(step, sender).wait_recv()
+        straight[rows_of(sender), :] = incoming[sender].astype(jnp.float32)
+        return carry
+
+    lax.fori_loop(0, tiles - 1, take_rows, 0)
+    lane_of = lax.broadcasted_iota(jnp.int32, chosen.shape, 1)
+
+    def make(target):
         def body(i, carry):
             for u in range(unroll):
                 j = i * unroll + u
-                key = listed[target, j // LANES, j % LANES]
-                picked[pl.ds(j, 1), :] = wide[pl.ds(key, 1), :]
+                row = source_ref[target * strip_capacity + j]
+                chosen[pl.ds(j, 1), :] = straight[pl.ds(row, 1), :]
             return carry
 
-        lax.fori_loop(0, capacity // unroll, body, 0)
-        outgoing[target] = picked[...].astype(jnp.bfloat16)
-
-    def send_rows(k, carry):
+        lax.fori_loop(0, strip_capacity // unroll, body, 0)
+        at = pl.ds(pl.multiple_of(target * strip_capacity, strip_capacity), strip_capacity)
+        kernel = chosen[...]
+        swapped = pltpu.roll(kernel, HALF, 1)
+        turned = jnp.where(lane_of < HALF, -swapped, swapped)
+        made = real_scale[at, :] * kernel + imag_scale[at, :] * turned
+        leaving[target] = made.astype(jnp.bfloat16)
+
+    def send_patches(k, carry):
         step = far_first(k, tiles)
-        look_up(peer(me, step, tiles))
-        row_copy(step, me).start()
-        return carry
-
-    lax.fori_loop(0, tiles - 1, send_rows, 0)
-    look_up(me)
-    keep = pltpu.make_async_copy(outgoing.at[me], rows_ref.at[me], own_sem)
+        make(peer(me, step, tiles))
+        patch_copy(step, me).start()
+        return carry
+
+    lax.fori_loop(0, tiles - 1, send_patches, 0)
+    make(me)
+    keep = pltpu.make_async_copy(leaving.at[me], patches_ref.at[me], own_sem)
     keep.start()
 
     def finish(step, carry):
         sender = peer(me, -step, tiles)
         note_copy(step, sender).wait_send()
-        row_copy(step, sender).wait()
+        row_copy(step, sender).wait_send()
+        patch_copy(step, sender).wait()
         return carry
 
     lax.fori_loop(1, tiles, finish, 0)
     keep.wait()
 
 
-def answer_requests(notes, table, tiles, capacity):
+def trade(source, notes, table, real, imag, tiles, phase_capacity, strip_capacity):
     width = table.shape[1]
     notes = notes.reshape(tiles, -1, LANES)
     vmem = pl.BlockSpec(memory_space=pltpu.VMEM)
+    hbm = pl.BlockSpec(memory_space=pl.ANY)
+    scales = pltpu.VMEM((tiles * strip_capacity, width), jnp.float32)
+    rows = pltpu.VMEM((tiles, phase_capacity, width), jnp.bfloat16)
+    each = pltpu.SemaphoreType.DMA((tiles,))
     return pl.pallas_call(
-        functools.partial(answer_kernel, tiles, capacity, 16),
+        functools.partial(trade_kernel, tiles, phase_capacity, strip_capacity, 16),
         out_shape=(
             jax.ShapeDtypeStruct(notes.shape, jnp.int32),
-            jax.ShapeDtypeStruct((tiles, capacity, width), jnp.bfloat16),
+            jax.ShapeDtypeStruct((tiles, strip_capacity, width), jnp.bfloat16),
         ),
-        in_specs=[vmem, vmem],
-        out_specs=(vmem, pl.BlockSpec(memory_space=pl.ANY)),
+        in_specs=[pl.BlockSpec(memory_space=pltpu.SMEM), vmem, hbm, vmem, vmem],
+        out_specs=(vmem, hbm),
         scratch_shapes=[
+            pltpu.VMEM(table.shape, jnp.bfloat16),
             pltpu.VMEM(table.shape, jnp.float32),
-            pltpu.VMEM((capacity, width), jnp.float32),
-            pltpu.VMEM((tiles, capacity, width), jnp.bfloat16),
+            pltpu.VMEM((phase_capacity, width), jnp.float32),
+            rows,
+            rows,
+            pltpu.VMEM((tiles * phase_capacity, width), jnp.float32),
+            scales,
+            scales,
+            pltpu.VMEM((strip_capacity, width), jnp.float32),
+            pltpu.VMEM((tiles, strip_capacity, width), jnp.bfloat16),
             pltpu.SMEM(notes.shape, jnp.int32),
-            pltpu.SemaphoreType.DMA((tiles,)),
-            pltpu.SemaphoreType.DMA((tiles,)),
-            pltpu.SemaphoreType.DMA((tiles,)),
-            pltpu.SemaphoreType.DMA((tiles,)),
+            each, each, each, each, each, each,
+            pltpu.SemaphoreType.DMA,
             pltpu.SemaphoreType.DMA,
         ],
         compiler_params=pltpu.CompilerParams(
             collective_id=0, has_side_effects=True, vmem_limit_bytes=40 * 2**20
         ),
-        name="answer_requests",
-    )(notes, table)
+        name="trade",
+    )(source.reshape(-1), notes, table, real, imag)
 
 
 def edges_kernel(
@@ -319,96 +381,6 @@
     )(other, own_edge, other_edge)
 
 
-def patch_kernel(
-    tiles, unroll, source_ref, real_ref, imag_ref, rows_ref, patches_ref,
-    wide, real_scale, imag_scale, picked, outgoing, sends, recvs, own_sem,
-):
-    me = lax.axis_index("tile")
-    barrier = greet_tiles(me, tiles)
-    wide[...] = rows_ref[...].astype(jnp.float32)
-
-    def scale(g, carry):
-        at = pl.ds(pl.multiple_of(g * LANES, LANES), LANES)
-        for values, scales in ((real_ref, real_scale), (imag_ref, imag_scale)):
-            scales[at, :] = jnp.broadcast_to(values[pl.ds(g, 1), :], (LANES, LANES)).T
-        return carry
-
-    lax.fori_loop(0, real_ref.shape[0], scale, 0)
-    pl.semaphore_wait(barrier, tiles - 1)
-    capacity = picked.shape[0]
-    lane = lax.broadcasted_iota(jnp.int32, picked.shape, 1)
-
-    def copy(step, sender):
-        target = peer(me, step, tiles)
-        return pltpu.make_async_remote_copy(
-            src_ref=outgoing.at[target],
-            dst_ref=patches_ref.at[sender],
-            send_sem=sends.at[step],
-            recv_sem=recvs.at[step],
-            device_id={"tile": target},
-            device_id_type=MESH,
-        )
-
-    def make(target):
-        def body(i, carry):
-            for u in range(unroll):
-                j = i * unroll + u
-                picked[pl.ds(j, 1), :] = wide[pl.ds(source_ref[target * capacity + j], 1), :]
-            return carry
-
-        lax.fori_loop(0, capacity // unroll, body, 0)
-        at = pl.ds(pl.multiple_of(target * capacity, capacity), capacity)
-        straight = picked[...]
-        swapped = pltpu.roll(straight, HALF, 1)
-        turned = jnp.where(lane < HALF, -swapped, swapped)
-        made = real_scale[at, :] * straight + imag_scale[at, :] * turned
-        outgoing[target] = made.astype(jnp.bfloat16)
-
-    def send(k, carry):
-        step = far_first(k, tiles)
-        make(peer(me, step, tiles))
-        copy(step, me).start()
-        return carry
-
-    lax.fori_loop(0, tiles - 1, send, 0)
-    make(me)
-    keep = pltpu.make_async_copy(outgoing.at[me], patches_ref.at[me], own_sem)
-    keep.start()
-
-    def finish(step, carry):
-        copy(step, peer(me, -step, tiles)).wait()
-        return carry
-
-    lax.fori_loop(1, tiles, finish, 0)
-    keep.wait()
-
-
-def send_patches(source, real, imag, rows, tiles):
-    slots, width = real.size, rows.shape[1]
-    capacity = slots // tiles
-    vmem = pl.BlockSpec(memory_space=pltpu.VMEM)
-    return pl.pallas_call(
-        functools.partial(patch_kernel, tiles, 16),
-        out_shape=jax.ShapeDtypeStruct((tiles, capacity, width), jnp.bfloat16),
-        in_specs=[pl.BlockSpec(memory_space=pltpu.SMEM), vmem, vmem, vmem],
-        out_specs=pl.BlockSpec(memory_space=pl.ANY),
-        scratch_shapes=[
-            pltpu.VMEM(rows.shape, jnp.float32),
-            pltpu.VMEM((slots, width), jnp.float32),
-            pltpu.VMEM((slots, width), jnp.float32),
-            pltpu.VMEM((capacity, width), jnp.float32),
-            pltpu.VMEM((tiles, capacity, width), jnp.bfloat16),
-            pltpu.SemaphoreType.DMA((tiles,)),
-            pltpu.SemaphoreType.DMA((tiles,)),
-            pltpu.SemaphoreType.DMA,
-        ],
-        compiler_params=pltpu.CompilerParams(
-            collective_id=2, has_side_effects=True, vmem_limit_bytes=40 * 2**20
-        ),
-        name="send_patches",
-    )(source.reshape(-1), real, imag, rows)
-
-
 def paint_kernel(
     unroll, cells_ref, band_ref, patches_ref, own_ref, own_edge_ref, other_ref, other_edge_ref, wide, *canvases
 ):
@@ -418,16 +390,18 @@
         ((source == target + s * SUP) & (target % HALF < SUP)).astype(jnp.bfloat16) for s in range(SUP)
     ]
 
+    chunk = math.gcd(patches_ref.shape[0], 1024)
+
     def open_out(i, carry):
-        first = pl.multiple_of(i * LANES, LANES)
-        part = patches_ref[pl.ds(first, LANES), :]
+        first = pl.multiple_of(i * chunk, chunk)
+        part = patches_ref[pl.ds(first, chunk), :]
         for s in range(SUP):
-            wide[pl.ds(first * SUP + s, LANES, stride=SUP), :] = jnp.dot(
+            wide[pl.ds(first * SUP + s, chunk, stride=SUP), :] = jnp.dot(
                 part, picks[s], preferred_element_type=jnp.float32
             )
         return carry
 
-    lax.fori_loop(0, patches_ref.shape[0] // LANES, open_out, 0)
+    lax.fori_loop(0, patches_ref.shape[0] // chunk, open_out, 0)
 
     def clear(i, carry):
         start = pl.multiple_of(i * HEIGHT, SUP)
@@ -498,7 +472,7 @@
             edge_ref[:, at] = jnp.concatenate(merged[-1], axis=0).astype(edge_ref.dtype)
             return carry
 
-        lax.fori_loop(0, blocks, column, 0)
+        lax.fori_loop(0, blocks, column, 0, unroll=4)
 
     band = band_ref[0]
     merge(band * blocks, own_ref, own_edge_ref)
@@ -512,7 +486,7 @@
     smem = pl.BlockSpec(memory_space=pltpu.SMEM)
     vmem = pl.BlockSpec(memory_space=pltpu.VMEM)
     return pl.pallas_call(
-        functools.partial(paint_kernel, 64),
+        functools.partial(paint_kernel, 128),
         out_shape=(main, edge, other, edge),
         in_specs=[smem, smem, vmem],
         out_specs=(vmem, vmem, vmem, vmem),
@@ -548,11 +522,11 @@
         sizes, band, plane_index, beam_index, strip_index, cell_row, cell_column, phase_index,
         visibility[:, 0], visibility[:, 1],
     )
-    got, rows = answer_requests(
-        notes, kernel_table.reshape(-1, row_width), strips, phase_capacity
+    got, patches = trade(
+        source, notes, kernel_table.reshape(-1, row_width), slot_real, slot_imag,
+        strips, phase_capacity, strip_capacity,
     )
     cells = got.reshape(strips, both)[:, phase_capacity:].reshape(-1)
-    patches = send_patches(source, slot_real, slot_imag, rows.reshape(-1, row_width), strips)
     patches = patches.reshape(-1, row_width)
 
     own, own_edge, other, other_edge = paint(cells, band, patches)

time: 130 us -> 109 us (0.84)
  Pallas kernels: 117 us -> 95.7 us
    pallas_call x3 -> x2, Pallas kernels: 104 us -> 82.6 us  [the longest x1 55.7 us: trade(): pl.pallas_call(functools.partial(trade_kernel, tiles, phase_capacity, str...]
where the time goes in v5:
time: 109 us; the launch traced here: 108 us
  Pallas kernels  95.7 us (88%)
  local copies, waits for them, and re-layouts  8.19 us (8%)
  other arithmetic  4.43 us (4%)
    pallas_call x1, Pallas kernels, trade(): pl.pallas_call(functools.partial(trade_kernel, tiles, phase_capacity, str...  55.7 us
    pallas_call x1, Pallas kernels, paint(): pl.pallas_call(functools.partial(paint_kernel, 128), out_shape=(main, edg...  26.9 us
    pallas_call x1, Pallas kernels, exchange_edges(): pl.pallas_call(functools.partial(edges_kernel, tiles, pieces), out_shape=...  11.6 us
    unnamed x19, local copies, waits for them, and re-layouts  7.38 us
    add x1, other arithmetic, local(): return own + received.astype(jnp.float32) + edge  3.42 us

profile of v5, /device:TPU:0, one launch (start us, length us, event | category | flops | bytes accessed | tf_op | source)
XLA Modules:
  0.0 108.3 jit_solution(17629372000624562584)
XLA Ops:
  0.0 0.8 fusion
  0.8 0.0 copy-start.2
  0.8 0.7 copy-done.2
  1.5 0.0 copy-start.3
  1.5 0.7 copy-done.3
  2.2 0.0 copy-start.4
  2.2 0.7 copy-done.4
  2.9 0.0 copy-start.5
  2.9 0.7 copy-done.5
  3.6 0.0 copy-start.6
  3.6 0.7 copy-done.6
  4.3 0.0 copy-start.7
  4.3 0.7 copy-done.7
  5.0 1.5 %addresses.1 = (s32[64,128]{1,0:T(8,128)S(1)}, s32[32,128]{1,0:T(8,128)S(1)}, f32[32,128]{1,0:T(8,128)S(1)}, f32[32,128]{1,0:T(8,128)S(1)}) custom-call(s32[1]{0:T(128)} %bitcast.band_ref, s32[16,128]{1,0:T(8,128)S(1)} %bitcast.29, s32[16,128]{1,0:T(8,128)S(1)} %bitcast.30, s32[16,128]{1,0:T(8,128)S(1)} %bitcast.31, s32[16,128]{1,0:T(8,128)S(1)} %bitcast.32, ...), custom_call_target="tpu_custom_call" | custom-call | tf_op jit(solution)/shard_map/addresses/pallas_call | solution.py:119
  6.5 0.0 copy-start
  6.5 1.6 %copy-done = bf16[32,32,8,128]{3,2,1,0:T(8,128)(2,1)S(1)} copy-done((bf16[32,32,8,128]{3,2,1,0:T(8,128)(2,1)S(1)}, bf16[32,32,8,128]{3,2,1,0:T(8,128)(2,1)}, u32[]{:S(2)}) %copy-start) | copy-done | bytes 2097176
  8.1 55.7 %trade.1 = (s32[8,8,128]{2,1,0:T(8,128)S(1)}, bf16[8,512,128]{2,1,0:T(8,128)(2,1)S(1)}) custom-call(s32[4096]{0:T(1024)S(1)} %bitcast.28, s32[8,8,128]{2,1,0:T(8,128)S(1)} %bitcast.24, bf16[8192,128]{1,0:T(8,128)(2,1)S(1)} %bitcast.22, f32[32,128]{1,0:T(8,128)S(1)} %get-tuple-element.20.real_ref, f32[32,128]{1,0:T(8,128)S(1)} %get-tuple-element.21.imag_ref), custom_call_target="tpu_custom_call" | custom-call | tf_op jit(solution)/shard_map/trade/pallas_call | solution.py:301
  63.8 0.0 copy-start.1
  63.8 1.0 copy-done.1
  64.8 0.6 copy.10
  65.4 26.9 %paint.1 = (f32[2,64,4096]{2,1,0:T(8,128)}, bf16[16,4096]{1,0:T(8,128)(2,1)}, bf16[2,64,4096]{2,1,0:T(8,128)(2,1)}, bf16[16,4096]{1,0:T(8,128)(2,1)}) custom-call(s32[4096]{0:T(1024)} %bitcast.36, s32[1]{0:T(128)} %bitcast.band_ref, bf16[4096,128]{1,0:T(8,128)(2,1)} %bitcast.23), custom_call_target="tpu_custom_call" | custom-call | tf_op jit(solution)/shard_map/paint/pallas_call | solution.py:488
  92.3 11.6 %exchange_edges.1 = (bf16[2,64,4096]{2,1,0:T(8,128)(2,1)}, bf16[16,4096]{1,0:T(8,128)(2,1)}, bf16[16,4096]{1,0:T(8,128)(2,1)}) custom-call(bf16[2,64,4096]{2,1,0:T(8,128)(2,1)} %get-tuple-element.25.other_ref, bf16[16,4096]{1,0:T(8,128)(2,1)} %get-tuple-element.26.own_edge_ref, bf16[16,4096]{1,0:T(8,128)(2,1)} %get-tuple-element.27.other_edge_ref), custom_call_target="tpu_custom_call" | custom-call | tf_op jit(solution)/shard_map/exchange_edges/pallas_call | solution.py:371
  103.9 1.0 select_bitcast_fusion
  104.9 3.4 %pad_add_fusion = f32[2,64,4096]{2,1,0:T(8,128)} fusion(f32[2,8,4096]{2,1,0:T(8,128)S(1)} %select_bitcast_fusion, f32[2,64,4096]{2,1,0:T(8,128)} %get-tuple-element.24, bf16[2,64,4096]{2,1,0:T(8,128)(2,1)} %get-tuple-element.28), kind=kLoop, calls=%fused_computation | loop fusion | flops 1572864 | bytes 5505024 | tf_op jit(solution)/shard_map/add | solution.py:537
  (2 shorter events, 0.0 us)
Async XLA Ops:
  0.8 0.7 copy-start.2
  1.5 0.7 copy-start.3
  2.2 0.7 copy-start.4
  2.9 0.7 copy-start.5
  3.6 0.7 copy-start.6
  4.3 0.7 copy-start.7
  6.5 1.6 %copy-start = (bf16[32,32,8,128]{3,2,1,0:T(8,128)(2,1)S(1)}, bf16[32,32,8,128]{3,2,1,0:T(8,128)(2,1)}, u32[]{:S(2)}) copy-start(bf16[32,32,8,128]{3,2,1,0:T(8,128)(2,1)} %param.15) | copy-start | bytes 6291460
  63.8 1.0 copy-start.1

commit v6 on v5

--- a/solution.py
+++ b/solution.py
@@ -126,7 +126,7 @@
         ),
         in_specs=[pl.BlockSpec(memory_space=pltpu.SMEM)] + [vmem] * len(columns),
         out_specs=(vmem,) * 4,
-        compiler_params=pltpu.CompilerParams(vmem_limit_bytes=40 * 2**20),
+        compiler_params=pltpu.CompilerParams(vmem_limit_bytes=58 * 2**20),
         name="addresses",
     )(band, *(column.reshape(blocks // LANES, LANES) for column in columns))
 
@@ -323,7 +323,7 @@
             pltpu.SemaphoreType.DMA,
         ],
         compiler_params=pltpu.CompilerParams(
-            collective_id=0, has_side_effects=True, vmem_limit_bytes=40 * 2**20
+            collective_id=0, has_side_effects=True, vmem_limit_bytes=58 * 2**20
         ),
         name="trade",
     )(source.reshape(-1), notes, table, real, imag)
@@ -376,7 +376,9 @@
         in_specs=[hbm] * 3,
         out_specs=(hbm,) * 3,
         scratch_shapes=[pltpu.SemaphoreType.DMA((count,)), pltpu.SemaphoreType.DMA((count,))],
-        compiler_params=pltpu.CompilerParams(collective_id=1, has_side_effects=True),
+        compiler_params=pltpu.CompilerParams(
+            collective_id=1, has_side_effects=True, vmem_limit_bytes=58 * 2**20
+        ),
         name="exchange_edges",
     )(other, own_edge, other_edge)
 
@@ -497,6 +499,30 @@
     )(cells, band, patches)
 
 
+def add_up_kernel(own_ref, received_ref, straight_ref, crossed_ref, out_ref):
+    total = own_ref[...] + received_ref[...].astype(jnp.float32)
+    edge = straight_ref[...].astype(jnp.float32) + crossed_ref[...].astype(jnp.float32)
+    edge = jnp.where(lax.axis_index("tile") > 0, edge, 0.0)
+    out_ref[...] = total
+    for k in range(2):
+        out_ref[k, :SUP, :] = total[k, :SUP] + edge[k * SUP : (k + 1) * SUP]
+
+
+def add_up(own, received, straight, crossed):
+    columns = 512
+    full = pl.BlockSpec((2, ROWS, columns), lambda c: (0, 0, c))
+    edge = pl.BlockSpec((2 * SUP, columns), lambda c: (0, c))
+    return pl.pallas_call(
+        add_up_kernel,
+        out_shape=jax.ShapeDtypeStruct(own.shape, own.dtype),
+        grid=(own.shape[2] // columns,),
+        in_specs=[full, full, edge, edge],
+        out_specs=full,
+        compiler_params=pltpu.CompilerParams(vmem_limit_bytes=58 * 2**20),
+        name="add_up",
+    )(own, received, straight, crossed)
+
+
 def local(
     visibility,
     plane_index,
@@ -531,10 +557,7 @@
 
     own, own_edge, other, other_edge = paint(cells, band, patches)
     received, straight, crossed = exchange_edges(strips, other, own_edge, other_edge)
-    edge = straight.astype(jnp.float32) + crossed.astype(jnp.float32)
-    edge = jnp.where(lax.axis_index("tile") > 0, edge, 0.0).reshape(2, SUP, -1)
-    edge = jnp.pad(edge, ((0, 0), (0, ROWS - SUP), (0, 0)))
-    return own + received.astype(jnp.float32) + edge
+    return add_up(own, received, straight, crossed)
 
 
 def solution(mesh):

time: 109 us -> 107 us (0.982)
  Pallas kernels: 95.7 us -> 104 us
  local copies, waits for them, and re-layouts: 8.19 us -> 2.79 us
  other arithmetic: 4.43 us -> 0 us
    pallas_call x0 -> x1, Pallas kernels: none -> 6.02 us  [add_up(): pl.pallas_call(add_up_kernel, out_shape=jax.ShapeDtypeStruct(own.shape, o...]
    unnamed x19 -> x3, local copies, waits for them, and re-layouts: 7.38 us -> 1.38 us
    add x1 -> x0, other arithmetic: 3.42 us -> none  [local(): return own + received.astype(jnp.float32) + edge]
    pallas_call x1, Pallas kernels: 1.52 us -> 2.93 us  [addresses(): pl.pallas_call(functools.partial(address_kernel, sizes), out_shape=(shape...]
where the time goes in v6:
time: 107 us
  Pallas kernels  104 us (97%)
  local copies, waits for them, and re-layouts  2.79 us (3%)
    pallas_call x1, Pallas kernels, trade(): pl.pallas_call(functools.partial(trade_kernel, tiles, phase_capacity, str...  56.6 us
    pallas_call x1, Pallas kernels, paint(): pl.pallas_call(functools.partial(paint_kernel, 128), out_shape=(main, edg...  27 us
    pallas_call x1, Pallas kernels, exchange_edges(): pl.pallas_call(functools.partial(edges_kernel, tiles, pieces), out_shape=...  11.3 us
    pallas_call x1, Pallas kernels, add_up(): pl.pallas_call(add_up_kernel, out_shape=jax.ShapeDtypeStruct(own.shape, o...  6.02 us
    pallas_call x1, Pallas kernels, addresses(): pl.pallas_call(functools.partial(address_kernel, sizes), out_shape=(shape...  2.93 us

profile of v6, /device:TPU:0, one launch (start us, length us, event | category | flops | bytes accessed | tf_op | source)
XLA Modules:
  0.0 106.7 jit_solution(1973502166568751043)
XLA Ops:
  0.0 1.4 %fusion = (f32[2048,1]{0,1:T(1,128)}, f32[2048,1]{0,1:T(1,128)}) fusion(f32[2048,2]{0,1:T(2,128)} %param.8), kind=kLoop, calls=%fused_computation.2 | loop fusion | bytes 32768 | tf_op jit(solution)/shard_map/slice | solution.py:549
  1.4 2.9 %addresses.1 = (s32[64,128]{1,0:T(8,128)}, s32[32,128]{1,0:T(8,128)}, f32[32,128]{1,0:T(8,128)}, f32[32,128]{1,0:T(8,128)}) custom-call(s32[1]{0:T(128)} %bitcast.band_ref, s32[16,128]{1,0:T(8,128)} %bitcast.29, s32[16,128]{1,0:T(8,128)} %bitcast.30, s32[16,128]{1,0:T(8,128)} %bitcast.31, s32[16,128]{1,0:T(8,128)} %bitcast.32, s32[16,128]{1,0:T(8,128)} %bitcast.33, ...), custom_call_target="tpu_custom_call" | custom-call | tf_op jit(solution)/shard_map/addresses/pallas_call | solution.py:119
  4.3 56.6 %trade.1 = (s32[8,8,128]{2,1,0:T(8,128)}, bf16[8,512,128]{2,1,0:T(8,128)(2,1)}) custom-call(s32[4096]{0:T(1024)} %bitcast.28, s32[8,8,128]{2,1,0:T(8,128)} %bitcast.24, bf16[8192,128]{1,0:T(8,128)(2,1)} %bitcast.20, f32[32,128]{1,0:T(8,128)} %get-tuple-element.20.real_ref, f32[32,128]{1,0:T(8,128)} %get-tuple-element.21.imag_ref), custom_call_target="tpu_custom_call" | custom-call | tf_op jit(solution)/shard_map/trade/pallas_call | solution.py:301
  61.0 0.8 copy.12
  61.7 0.6 copy.10
  62.4 27.0 %paint.1 = (f32[2,64,4096]{2,1,0:T(8,128)}, bf16[16,4096]{1,0:T(8,128)(2,1)}, bf16[2,64,4096]{2,1,0:T(8,128)(2,1)}, bf16[16,4096]{1,0:T(8,128)(2,1)}) custom-call(s32[4096]{0:T(1024)} %bitcast.23, s32[1]{0:T(128)} %bitcast.band_ref, bf16[4096,128]{1,0:T(8,128)(2,1)} %bitcast.21), custom_call_target="tpu_custom_call" | custom-call | tf_op jit(solution)/shard_map/paint/pallas_call | solution.py:490
  89.3 11.3 %exchange_edges.1 = (bf16[2,64,4096]{2,1,0:T(8,128)(2,1)}, bf16[16,4096]{1,0:T(8,128)(2,1)}, bf16[16,4096]{1,0:T(8,128)(2,1)}) custom-call(bf16[2,64,4096]{2,1,0:T(8,128)(2,1)} %get-tuple-element.25.other_ref, bf16[16,4096]{1,0:T(8,128)(2,1)} %get-tuple-element.26.own_edge_ref, bf16[16,4096]{1,0:T(8,128)(2,1)} %get-tuple-element.27.other_edge_ref), custom_call_target="tpu_custom_call" | custom-call | tf_op jit(solution)/shard_map/exchange_edges/pallas_call | solution.py:371
  100.6 6.0 %add_up.1 = f32[2,64,4096]{2,1,0:T(8,128)} custom-call(f32[2,64,4096]{2,1,0:T(8,128)} %get-tuple-element.24.own_ref, bf16[2,64,4096]{2,1,0:T(8,128)(2,1)} %get-tuple-element.28.received_ref, bf16[16,4096]{1,0:T(8,128)(2,1)} %get-tuple-element.29.straight_ref, bf16[16,4096]{1,0:T(8,128)(2,1)} %get-tuple-element.30.crossed_ref), custom_call_target="tpu_custom_call" | custom-call | tf_op jit(solution)/shard_map/add_up/pallas_call | solution.py:515
  (1 shorter events, 0.0 us)

commit v7 on v6

--- a/solution.py
+++ b/solution.py
@@ -500,24 +500,26 @@
 
 
 def add_up_kernel(own_ref, received_ref, straight_ref, crossed_ref, out_ref):
-    total = own_ref[...] + received_ref[...].astype(jnp.float32)
-    edge = straight_ref[...].astype(jnp.float32) + crossed_ref[...].astype(jnp.float32)
-    edge = jnp.where(lax.axis_index("tile") > 0, edge, 0.0)
-    out_ref[...] = total
-    for k in range(2):
-        out_ref[k, :SUP, :] = total[k, :SUP] + edge[k * SUP : (k + 1) * SUP]
+    out_ref[...] = own_ref[...] + received_ref[...].astype(jnp.float32)
+    lower_edge = (pl.program_id(1) == 0) & (lax.axis_index("tile") > 0)
+
+    @pl.when(lower_edge)
+    def _():
+        edge = straight_ref[...].astype(jnp.float32) + crossed_ref[...].astype(jnp.float32)
+        edge = jnp.where(pl.program_id(0) == 0, edge[:SUP], edge[SUP:])
+        out_ref[0, :SUP, :] = out_ref[0, :SUP, :] + edge
 
 
 def add_up(own, received, straight, crossed):
-    columns = 512
-    full = pl.BlockSpec((2, ROWS, columns), lambda c: (0, 0, c))
-    edge = pl.BlockSpec((2 * SUP, columns), lambda c: (0, c))
+    rows, columns = ROWS // 2, own.shape[2]
+    part = pl.BlockSpec((1, rows, columns), lambda k, r: (k, r, 0))
+    edge = pl.BlockSpec((2 * SUP, columns), lambda k, r: (0, 0))
     return pl.pallas_call(
         add_up_kernel,
         out_shape=jax.ShapeDtypeStruct(own.shape, own.dtype),
-        grid=(own.shape[2] // columns,),
-        in_specs=[full, full, edge, edge],
-        out_specs=full,
+        grid=(2, ROWS // rows),
+        in_specs=[part, part, edge, edge],
+        out_specs=part,
         compiler_params=pltpu.CompilerParams(vmem_limit_bytes=58 * 2**20),
         name="add_up",
     )(own, received, straight, crossed)

time: 107 us -> 105 us (0.981)
  Pallas kernels: 104 us -> 102 us
    pallas_call x1, Pallas kernels: 6.02 us -> 4.05 us  [add_up(): pl.pallas_call(add_up_kernel, out_shape=jax.ShapeDtypeStruct(own.shape, o...]
where the time goes in v7:
time: 105 us
  Pallas kernels  102 us (97%)
  local copies, waits for them, and re-layouts  2.79 us (3%)
    pallas_call x1, Pallas kernels, trade(): pl.pallas_call(functools.partial(trade_kernel, tiles, phase_capacity, str...  56.6 us
    pallas_call x1, Pallas kernels, paint(): pl.pallas_call(functools.partial(paint_kernel, 128), out_shape=(main, edg...  27 us
    pallas_call x1, Pallas kernels, exchange_edges(): pl.pallas_call(functools.partial(edges_kernel, tiles, pieces), out_shape=...  11.5 us
    pallas_call x1, Pallas kernels, add_up(): pl.pallas_call(add_up_kernel, out_shape=jax.ShapeDtypeStruct(own.shape, o...  4.05 us
    pallas_call x1, Pallas kernels, addresses(): pl.pallas_call(functools.partial(address_kernel, sizes), out_shape=(shape...  2.93 us

profile of v7, /device:TPU:0, one launch (start us, length us, event | category | flops | bytes accessed | tf_op | source)
XLA Modules:
  0.0 104.9 jit_solution(3933425713332522867)
XLA Ops:
  0.0 1.4 %fusion = (f32[2048,1]{0,1:T(1,128)}, f32[2048,1]{0,1:T(1,128)}) fusion(f32[2048,2]{0,1:T(2,128)} %param.8), kind=kLoop, calls=%fused_computation.2 | loop fusion | bytes 32768 | tf_op jit(solution)/shard_map/slice | solution.py:551
  1.4 2.9 %addresses.1 = (s32[64,128]{1,0:T(8,128)}, s32[32,128]{1,0:T(8,128)}, f32[32,128]{1,0:T(8,128)}, f32[32,128]{1,0:T(8,128)}) custom-call(s32[1]{0:T(128)} %bitcast.band_ref, s32[16,128]{1,0:T(8,128)} %bitcast.29, s32[16,128]{1,0:T(8,128)} %bitcast.30, s32[16,128]{1,0:T(8,128)} %bitcast.31, s32[16,128]{1,0:T(8,128)} %bitcast.32, s32[16,128]{1,0:T(8,128)} %bitcast.33, ...), custom_call_target="tpu_custom_call" | custom-call | tf_op jit(solution)/shard_map/addresses/pallas_call | solution.py:119
  4.3 56.6 %trade.1 = (s32[8,8,128]{2,1,0:T(8,128)}, bf16[8,512,128]{2,1,0:T(8,128)(2,1)}) custom-call(s32[4096]{0:T(1024)} %bitcast.28, s32[8,8,128]{2,1,0:T(8,128)} %bitcast.24, bf16[8192,128]{1,0:T(8,128)(2,1)} %bitcast.20, f32[32,128]{1,0:T(8,128)} %get-tuple-element.20.real_ref, f32[32,128]{1,0:T(8,128)} %get-tuple-element.21.imag_ref), custom_call_target="tpu_custom_call" | custom-call | tf_op jit(solution)/shard_map/trade/pallas_call | solution.py:301
  61.0 0.8 copy.12
  61.7 0.6 copy.10
  62.4 27.0 %paint.1 = (f32[2,64,4096]{2,1,0:T(8,128)}, bf16[16,4096]{1,0:T(8,128)(2,1)}, bf16[2,64,4096]{2,1,0:T(8,128)(2,1)}, bf16[16,4096]{1,0:T(8,128)(2,1)}) custom-call(s32[4096]{0:T(1024)} %bitcast.23, s32[1]{0:T(128)} %bitcast.band_ref, bf16[4096,128]{1,0:T(8,128)(2,1)} %bitcast.21), custom_call_target="tpu_custom_call" | custom-call | tf_op jit(solution)/shard_map/paint/pallas_call | solution.py:490
  89.3 11.5 %exchange_edges.1 = (bf16[2,64,4096]{2,1,0:T(8,128)(2,1)}, bf16[16,4096]{1,0:T(8,128)(2,1)}, bf16[16,4096]{1,0:T(8,128)(2,1)}) custom-call(bf16[2,64,4096]{2,1,0:T(8,128)(2,1)} %get-tuple-element.25.other_ref, bf16[16,4096]{1,0:T(8,128)(2,1)} %get-tuple-element.26.own_edge_ref, bf16[16,4096]{1,0:T(8,128)(2,1)} %get-tuple-element.27.other_edge_ref), custom_call_target="tpu_custom_call" | custom-call | tf_op jit(solution)/shard_map/exchange_edges/pallas_call | solution.py:371
  100.9 4.0 %add_up.1 = f32[2,64,4096]{2,1,0:T(8,128)} custom-call(f32[2,64,4096]{2,1,0:T(8,128)} %get-tuple-element.24.own_ref, bf16[2,64,4096]{2,1,0:T(8,128)(2,1)} %get-tuple-element.28.received_ref, bf16[16,4096]{1,0:T(8,128)(2,1)} %get-tuple-element.29.straight_ref, bf16[16,4096]{1,0:T(8,128)(2,1)} %get-tuple-element.30.crossed_ref), custom_call_target="tpu_custom_call" | custom-call | tf_op jit(solution)/shard_map/add_up/pallas_call | solution.py:517
  (1 shorter events, 0.0 us)
